TPU v7x, 256 devices: a whole 4x4x8 slice. The times are simulated.
256 devices in a mesh: seq: 32 (over x_lo, z, core), head: 8 (over y, x_hi).
Axes of the slice: x: 4 (x_hi: 2, x_lo: 2; x = x_hi * 2 + x_lo), y: 4, z: 8, core: 2. Of those that a mesh axis runs over, the one named last changes fastest.
Arguments:
- queries: bfloat16 [16384, 4096], P(('seq', 'head')), may hold values from -12.75 to 12.75
- keys: bfloat16 [16384, 1024], P(('seq', 'head')), may hold values from -9 to 9
- values: bfloat16 [16384, 1024], P(('seq', 'head')), may hold values from -6 to 6
- output_gradient: bfloat16 [16384, 4096], P(('seq', 'head')), may hold values from -6 to 6
- outputs: bfloat16 [16384, 4096], P(('seq', 'head')), may hold values from -2 to 2
- block_order: int32 [64], replicated, may hold values from 0 to 63, as said below
- doc_start: int32 [64], replicated, may hold values 0 or 1
Outputs:
- grad_queries: bfloat16 [16384, 4096], P(('seq', 'head'))
- key_gradients: bfloat16 [16384, 1024], P(('seq', 'head'))
- value_gradients: bfloat16 [16384, 1024], P(('seq', 'head'))
Inputs may be any that keep to these rules, and one draw needn't show every extreme that they name: `block_order`: for one c and every slab s, slots 2 s and 2 s + 1 hold, in either order, blocks b and 63 - b with b = (s + c) mod 32.
All inputs are finite; a program needn't handle non-finite values.
Results may differ from a plain program's by a relative error of at most 0.007.
Values may be sent and summed in bfloat16 or wider, within the bound.
No kernel may reach another device: no remote copies, remote signals or barrier semaphores. Data moves between devices by JAX's collectives and lax.ppermute only.
A program may use at most 128 MiB of HBM per device.

v0:
```python
import functools
import math

import jax
import jax.numpy as jnp
from jax import lax
from jax.experimental import pallas as pl
from jax.experimental.pallas import tpu as pltpu
from jax.sharding import PartitionSpec as P

QUERY_HEADS = 32
KEY_VALUE_HEADS = 8
GROUP = QUERY_HEADS // KEY_VALUE_HEADS
HEAD = 128
REACH = 2
WINDOW = 2 * REACH + 1
BLK = 256
SCALE = 1.0 / math.sqrt(HEAD)
SCALE2 = SCALE * math.log2(math.e)
MASKED = -1e30
DELTA_ROWS = 16


def send(value, steps):
    count = lax.axis_size("seq")
    return lax.ppermute(value, "seq", [(i, (i + steps) % count) for i in range(count)])


def swap_heads(value):
    return lax.all_to_all(value, "head", split_axis=0, concat_axis=0, tiled=True)


def pack_kernel(owners, q_ref, g_ref, o_ref, k_ref, v_ref, kv_ref, qg_ref):
    rows = q_ref.shape[0]
    width = GROUP * HEAD
    for n in range(owners):
        kv_ref[n, :, :HEAD] = k_ref[:, n * HEAD : (n + 1) * HEAD]
        kv_ref[n, :, HEAD:] = v_ref[:, n * HEAD : (n + 1) * HEAD]
        deltas = []
        for h in range(GROUP):
            cols = slice(n * width + h * HEAD, n * width + (h + 1) * HEAD)
            grad = g_ref[:, cols]
            qg_ref[n, h * rows : (h + 1) * rows, :] = q_ref[:, cols]
            qg_ref[n, (GROUP + h) * rows : (GROUP + h + 1) * rows, :] = grad
            deltas.append(grad.astype(jnp.float32) * o_ref[:, cols].astype(jnp.float32))
        lines = []
        for h in range(0, GROUP, 2):
            both = jnp.concatenate(deltas[h : h + 2], axis=0)
            lines.append(jnp.sum(both.T, axis=0, keepdims=True))
        delta = jnp.concatenate(lines, axis=0)
        high = delta.astype(jnp.bfloat16).astype(jnp.float32)
        spare = jnp.zeros((DELTA_ROWS - 2 * GROUP // 2, HEAD), jnp.float32)
        tile = jnp.concatenate([high, delta - high, spare], axis=0)
        qg_ref[n, 2 * GROUP * rows :, :] = tile.astype(jnp.bfloat16)


def pack(queries, keys, values, grads, outputs, heads):
    rows = queries.shape[0]
    owners = 2
    wide = pl.BlockSpec((rows, owners * GROUP * HEAD), lambda n: (0, n))
    narrow = pl.BlockSpec((rows, owners * HEAD), lambda n: (0, n))
    qg_rows = 2 * GROUP * rows + DELTA_ROWS
    return pl.pallas_call(
        functools.partial(pack_kernel, owners),
        grid=(heads // owners,),
        in_specs=[wide, wide, wide, narrow, narrow],
        out_specs=[
            pl.BlockSpec((owners, rows, 2 * HEAD), lambda n: (n, 0, 0)),
            pl.BlockSpec((owners, qg_rows, HEAD), lambda n: (n, 0, 0)),
        ],
        out_shape=[
            jax.ShapeDtypeStruct((heads, rows, 2 * HEAD), jnp.bfloat16),
            jax.ShapeDtypeStruct((heads, qg_rows, HEAD), jnp.bfloat16),
        ],
        name="pack",
    )(queries, grads, outputs, keys, values)


def attention_kernel(
    seq_size, mine_ref, order_ref, start_ref, qg_ref, *refs
):
    kv_refs = refs[:WINDOW]
    dq_ref = refs[WINDOW]
    dkv_refs = refs[WINDOW + 1 : 2 * WINDOW + 1]
    docs_ref, keep_ref, kv, scores, qt, gt, dqt, dkv, stats, sems = refs[2 * WINDOW + 1 :]
    sources = qg_ref.shape[0]
    rows = (qg_ref.shape[1] - DELTA_ROWS) // (2 * GROUP)
    chunk = GROUP * rows
    per_block = BLK // rows
    slots = 2 * WINDOW
    own = 2 * REACH

    copies = [
        pltpu.make_async_copy(kv_refs[n], kv.at[pl.ds(n * 2 * BLK, 2 * BLK)], sems.at[n])
        for n in range(WINDOW)
    ]
    for copy in copies:
        copy.start()

    def count(b, running):
        running = running + jnp.where(b > 0, start_ref[b], 0)
        docs_ref[b] = running
        return running

    lax.fori_loop(0, order_ref.shape[0], count, jnp.int32(0))
    mine = mine_ref[0]
    blocks = []
    for j in range(slots):
        slab = lax.rem(mine + (j // 2 - REACH) + seq_size, seq_size)
        blocks.append(order_ref[2 * slab + j % 2])
    for i in range(2):
        for j in range(slots):
            kept = (blocks[j] <= blocks[own + i]) & (docs_ref[blocks[j]] == docs_ref[blocks[own + i]])
            keep_ref[i * slots + j] = kept.astype(jnp.int32)

    for i in range(2):
        for c in range(per_block):
            source = i * per_block + c
            qt[i, :, c * chunk : (c + 1) * chunk] = qg_ref[source, :chunk, :].T
            gt[i, :, c * chunk : (c + 1) * chunk] = qg_ref[source, chunk : 2 * chunk, :].T
    dkv[...] = jnp.zeros_like(dkv)
    for copy in copies:
        copy.wait()

    def keys_of(j):
        return kv[pl.ds(pl.multiple_of(j * BLK, BLK), BLK), :HEAD]

    def values_of(j):
        return kv[pl.ds(pl.multiple_of(j * BLK, BLK), BLK), HEAD:]

    def score(i, j, diagonal):
        keys = keys_of(j)
        for c in range(per_block):
            lanes = slice(c * chunk, (c + 1) * chunk)
            s = jnp.dot(keys, qt[i, :, lanes], preferred_element_type=jnp.float32)
            if diagonal:
                key_at = lax.broadcasted_iota(jnp.int32, (BLK, chunk), 0)
                query_at = c * rows + lax.broadcasted_iota(jnp.int32, (BLK, chunk), 1) % rows
                s = jnp.where(key_at <= query_at, s, MASKED)
            scores[j, :, lanes] = s
            top = jnp.max(s, axis=0, keepdims=True)
            if diagonal:
                stats[0:1, lanes] = top
                stats[1:2, lanes] = jnp.sum(jnp.exp2((s - top) * SCALE2), axis=0, keepdims=True)
            else:
                before = stats[0:1, lanes]
                top = jnp.maximum(top, before)
                stats[0:1, lanes] = top
                stats[1:2, lanes] = stats[1:2, lanes] * jnp.exp2((before - top) * SCALE2) + jnp.sum(
                    jnp.exp2((s - top) * SCALE2), axis=0, keepdims=True
                )

    def gradients(i, j, first):
        keys = keys_of(j)
        values = values_of(j)
        add_k = None
        add_v = None
        for c in range(per_block):
            source = i * per_block + c
            lanes = slice(c * chunk, (c + 1) * chunk)
            probs = jnp.exp2(scores[j, :, lanes] * SCALE2 - stats[2:3, lanes])
            dprobs = jnp.dot(values, gt[i, :, lanes], preferred_element_type=jnp.float32)
            dscores = ((SCALE * probs) * (dprobs - stats[3:4, lanes])).astype(jnp.bfloat16)
            probs = probs.astype(jnp.bfloat16)
            v = jnp.dot(probs, qg_ref[source, chunk : 2 * chunk, :], preferred_element_type=jnp.float32)
            k = jnp.dot(dscores, qg_ref[source, :chunk, :], preferred_element_type=jnp.float32)
            add_v = v if add_v is None else add_v + v
            add_k = k if add_k is None else add_k + k
            q = lax.dot_general(
                keys, dscores, (((0,), (0,)), ((), ())), preferred_element_type=jnp.float32
            )
            dqt[:, lanes] = q if first else dqt[:, lanes] + q
        here = pl.ds(pl.multiple_of(j * BLK, BLK), BLK)
        dkv[here, :HEAD] += add_k
        dkv[here, HEAD:] += add_v

    for i in range(2):
        for c in range(per_block):
            base = 2 * chunk
            source = i * per_block + c
            tile = qg_ref[source, base:, :].astype(jnp.float32)
            delta = tile[0:2, :] + tile[2:4, :]
            stats[3:4, c * chunk : c * chunk + HEAD] = delta[0:1, :]
            stats[3:4, c * chunk + HEAD : (c + 1) * chunk] = delta[1:2, :]
        score(i, own + i, True)

        def visit_scores(j, _):
            @pl.when((keep_ref[i * slots + j] == 1) & (j != own + i))
            def _():
                score(i, j, False)

            return 0

        lax.fori_loop(0, slots, visit_scores, 0)
        stats[2:3, :] = stats[0:1, :] * SCALE2 + jnp.log2(stats[1:2, :])
        gradients(i, own + i, True)

        def visit_gradients(j, _):
            @pl.when((keep_ref[i * slots + j] == 1) & (j != own + i))
            def _():
                gradients(i, j, False)

            return 0

        lax.fori_loop(0, slots, visit_gradients, 0)
        for c in range(per_block):
            dq_ref[i * per_block + c] = dqt[:, c * chunk : (c + 1) * chunk].T.astype(jnp.bfloat16)

    for n in range(WINDOW):
        dkv_refs[n][...] = dkv[n * 2 * BLK : (n + 1) * 2 * BLK, :].astype(dkv_refs[n].dtype)


def attention(mine, block_order, doc_start, qg, kvs, seq_size):
    sources, qg_rows, _ = qg.shape
    rows = (qg_rows - DELTA_ROWS) // (2 * GROUP)
    slab = sources * rows
    lanes = BLK * GROUP
    smem = pl.BlockSpec(memory_space=pltpu.SMEM)
    vmem = pl.BlockSpec(memory_space=pltpu.VMEM)
    return pl.pallas_call(
        functools.partial(attention_kernel, seq_size),
        in_specs=[smem, smem, smem, vmem] + [pl.BlockSpec(memory_space=pl.ANY)] * WINDOW,
        out_specs=[vmem] * (1 + WINDOW),
        out_shape=[jax.ShapeDtypeStruct((sources, GROUP * rows, HEAD), jnp.bfloat16)]
        + [
            jax.ShapeDtypeStruct((slab, 2 * HEAD), jnp.float32 if n == REACH else jnp.bfloat16)
            for n in range(WINDOW)
        ],
        scratch_shapes=[
            pltpu.SMEM((block_order.shape[0],), jnp.int32),
            pltpu.SMEM((4 * WINDOW,), jnp.int32),
            pltpu.VMEM((WINDOW * slab, 2 * HEAD), jnp.bfloat16),
            pltpu.VMEM((2 * WINDOW, BLK, lanes), jnp.float32),
            pltpu.VMEM((2, HEAD, lanes), jnp.bfloat16),
            pltpu.VMEM((2, HEAD, lanes), jnp.bfloat16),
            pltpu.VMEM((HEAD, lanes), jnp.float32),
            pltpu.VMEM((WINDOW * slab, 2 * HEAD), jnp.float32),
            pltpu.VMEM((8, lanes), jnp.float32),
            pltpu.SemaphoreType.DMA((WINDOW,)),
        ],
        compiler_params=pltpu.CompilerParams(vmem_limit_bytes=40 * 1024 * 1024),
        cost_estimate=pl.CostEstimate(flops=3_000_000_000, bytes_accessed=4_000_000, transcendentals=8_000_000),
        name="attention",
    )(mine, block_order, doc_start, qg, *kvs)


def local(queries, keys, values, output_gradient, outputs, block_order, doc_start):
    heads = lax.axis_size("head")
    seq_size = lax.axis_size("seq")
    rows = queries.shape[0]
    kv, qg = pack(queries, keys, values, output_gradient, outputs, heads)
    kv = swap_heads(kv).reshape(heads * rows, 2 * HEAD)
    qg = swap_heads(qg)
    kvs = [kv if n == REACH else send(kv, REACH - n) for n in range(WINDOW)]
    mine = lax.axis_index("seq").astype(jnp.int32).reshape(1)
    dq, *dkvs = attention(mine, block_order, doc_start, qg, kvs, seq_size)
    total = dkvs[REACH]
    for n in range(WINDOW):
        if n != REACH:
            total = total + send(dkvs[n], n - REACH).astype(jnp.float32)
    dq = swap_heads(dq)
    dkv = swap_heads(total.astype(jnp.bfloat16).reshape(heads, rows, 2 * HEAD))
    dq = dq.reshape(heads, GROUP, rows, HEAD).transpose(2, 0, 1, 3).reshape(rows, heads * GROUP * HEAD)
    dk = dkv[:, :, :HEAD].transpose(1, 0, 2).reshape(rows, heads * HEAD)
    dv = dkv[:, :, HEAD:].transpose(1, 0, 2).reshape(rows, heads * HEAD)
    return dq, dk, dv


def solution(mesh):
    rows = P(("seq", "head"), None)
    return jax.shard_map(
        local,
        mesh=mesh,
        in_specs=(rows, rows, rows, rows, rows, P(), P()),
        out_specs=(rows, rows, rows),
        check_vma=False,
    )
```

profile of v0, /device:TPU:2, one launch (start us, length us, event | category | flops | bytes accessed | tf_op | source)
XLA Modules:
  0.0 103.8 jit_solution(9694239722202783841)
XLA Ops:
  0.6 3.9 %pack.1 = (bf16[8,64,256]{2,1,0:T(8,128)(2,1)}, bf16[8,528,128]{2,1,0:T(8,128)(2,1)}) custom-call(bf16[64,4096]{1,0:T(8,128)(2,1)} %q_ref.1, bf16[64,4096]{1,0:T(8,128)(2,1)} %g_ref.1, bf16[64,4096]{1,0:T(8,128)(2,1)} %o_ref.1, bf16[64,1024]{1,0:T(8,128)(2,1)} %k_ref.1, bf16[64,1024]{1,0:T(8,128)(2,1)} %v_ref.1), custom_call_target="tpu_custom_call" | custom-call | tf_op jit(solution)/shard_map/pack/pallas_call | solution.py:63
  4.5 14.8 %all_to_all.20 = bf16[8,64,256]{2,1,0:T(8,128)(2,1)S(1)} all-to-all(bf16[8,64,256]{2,1,0:T(8,128)(2,1)} %get-tuple-element.12), channel_id=1, replica_groups=mesh['seq'=32,'head'=8] {'head'}, dimensions={0} | all-to-all | bytes 524288 | tf_op jit(solution)/shard_map/all_to_all | solution.py:30
  19.3 3.7 %all-to-all-start = ((bf16[8,528,128]{2,1,0:T(8,128)(2,1)}), bf16[8,528,128]{2,1,0:T(8,128)(2,1)S(1)}, u32[]{:S(2)}, u32[]{:S(2)}) async-start(bf16[8,528,128]{2,1,0:T(8,128)(2,1)} %get-tuple-element.11), calls=%async_computation | async-start | bytes 2162688 | tf_op jit(solution)/shard_map/all_to_all | solution.py:30
  23.0 6.8 %collective-permute-start.3 = (bf16[512,256]{1,0:T(8,128)(2,1)S(1)}, bf16[512,256]{1,0:T(8,128)(2,1)S(1)}, u32[]{:S(2)}, u32[]{:S(2)}) collective-permute-start(bf16[512,256]{1,0:T(8,128)(2,1)S(1)} %bitcast.16), channel_id=1, source_target_pairs={{0,240},{8,248},{16,0},{24,8},{32,16},{40,24},{48,32},{56,40},{64,... | collective-permute-start | bytes 786440 | tf_op jit(solution)/shard_map/ppermute | solution.py:26
  29.8 0.5 collective-permute-start.1
  30.3 3.7 %collective-permute-done.3.refs_4_ = bf16[512,256]{1,0:T(8,128)(2,1)S(1)} collective-permute-done((bf16[512,256]{1,0:T(8,128)(2,1)S(1)}, bf16[512,256]{1,0:T(8,128)(2,1)S(1)}, u32[]{:S(2)}, u32[]{:S(2)}) %collective-permute-start.3) | collective-permute-done | bytes 262176 | tf_op jit(solution)/shard_map/ppermute | solution.py:26
  34.0 2.8 %collective-permute-done.2.refs_3_ = bf16[512,256]{1,0:T(8,128)(2,1)S(1)} collective-permute-done((bf16[512,256]{1,0:T(8,128)(2,1)S(1)}, bf16[512,256]{1,0:T(8,128)(2,1)S(1)}, u32[]{:S(2)}, u32[]{:S(2)}) %collective-permute-start.2) | collective-permute-done | bytes 262176 | tf_op jit(solution)/shard_map/ppermute | solution.py:26
  36.8 2.7 %collective-permute-done.1.refs_1_ = bf16[512,256]{1,0:T(8,128)(2,1)S(1)} collective-permute-done((bf16[512,256]{1,0:T(8,128)(2,1)S(1)}, bf16[512,256]{1,0:T(8,128)(2,1)S(1)}, u32[]{:S(2)}, u32[]{:S(2)}) %collective-permute-start.1) | collective-permute-done | bytes 262176 | tf_op jit(solution)/shard_map/ppermute | solution.py:26
  39.5 2.2 %collective-permute-done.refs_0_ = bf16[512,256]{1,0:T(8,128)(2,1)S(1)} collective-permute-done((bf16[512,256]{1,0:T(8,128)(2,1)S(1)}, bf16[512,256]{1,0:T(8,128)(2,1)S(1)}, u32[]{:S(2)}, u32[]{:S(2)}) %collective-permute-start) | collective-permute-done | bytes 262176 | tf_op jit(solution)/shard_map/ppermute | solution.py:26
  41.7 6.1 %all-to-all-done.qg_ref = bf16[8,528,128]{2,1,0:T(8,128)(2,1)S(1)} async-done(((bf16[8,528,128]{2,1,0:T(8,128)(2,1)}), bf16[8,528,128]{2,1,0:T(8,128)(2,1)S(1)}, u32[]{:S(2)}, u32[]{:S(2)}) %all-to-all-start) | async-done | bytes 1081376 | tf_op jit(solution)/shard_map/all_to_all | solution.py:30
  47.8 11.8 %attention.1 = (bf16[8,256,128]{2,1,0:T(8,128)(2,1)}, bf16[512,256]{1,0:T(8,128)(2,1)}, bf16[512,256]{1,0:T(8,128)(2,1)}, f32[512,256]{1,0:T(8,128)S(1)}, bf16[5...) custom-call(s32[1]{0:T(128)} %bitcast.mine_ref, s32[64]{0:T(128)S(1)} %copy-done, s32[64]{0:T(128)S(1)} %copy-done.1, ...), custom_call_target="tpu_custom_call" | custom-call | flops 3000000000 | bytes 4000000 | tf_op jit(solution)/shard_map/attention/pallas_call | solution.py:220
  59.6 6.8 %collective-permute-start.4 = (bf16[512,256]{1,0:T(8,128)(2,1)}, bf16[512,256]{1,0:T(8,128)(2,1)S(1)}, u32[]{:S(2)}, u32[]{:S(2)}) collective-permute-start(bf16[512,256]{1,0:T(8,128)(2,1)} %get-tuple-element.15), channel_id=1, source_target_pairs={{0,240},{8,248},{16,0},{24,8},{32,16},{40,24},{48,32},{56,40},{64,... | collective-permute-start | bytes 786440 | tf_op jit(solution)/shard_map/ppermute | solution.py:26
  66.4 0.5 collective-permute-start.6
  66.9 3.5 %all-to-all-start.2 = ((bf16[8,256,128]{2,1,0:T(8,128)(2,1)}), bf16[8,256,128]{2,1,0:T(8,128)(2,1)S(1)}, u32[]{:S(2)}, u32[]{:S(2)}) async-start(bf16[8,256,128]{2,1,0:T(8,128)(2,1)} %get-tuple-element.13), calls=%async_computation.2 | async-start | bytes 1048576 | tf_op jit(solution)/shard_map/all_to_all | solution.py:30
  70.6 2.8 %collective-permute-done.5 = bf16[512,256]{1,0:T(8,128)(2,1)S(1)} collective-permute-done((bf16[512,256]{1,0:T(8,128)(2,1)}, bf16[512,256]{1,0:T(8,128)(2,1)S(1)}, u32[]{:S(2)}, u32[]{:S(2)}) %collective-permute-start.5) | collective-permute-done | bytes 262176 | tf_op jit(solution)/shard_map/ppermute | solution.py:26
  73.4 2.6 %collective-permute-done.6 = bf16[512,256]{1,0:T(8,128)(2,1)S(1)} collective-permute-done((bf16[512,256]{1,0:T(8,128)(2,1)S(1)}, bf16[512,256]{1,0:T(8,128)(2,1)S(1)}, u32[]{:S(2)}, u32[]{:S(2)}) %collective-permute-start.6) | collective-permute-done | bytes 262176 | tf_op jit(solution)/shard_map/ppermute | solution.py:26
  76.0 2.2 %collective-permute-done.7 = bf16[512,256]{1,0:T(8,128)(2,1)S(1)} collective-permute-done((bf16[512,256]{1,0:T(8,128)(2,1)S(1)}, bf16[512,256]{1,0:T(8,128)(2,1)S(1)}, u32[]{:S(2)}, u32[]{:S(2)}) %collective-permute-start.7) | collective-permute-done | bytes 262176 | tf_op jit(solution)/shard_map/ppermute | solution.py:26
  78.2 0.9 add_convert_fusion
  79.1 11.7 %all-to-all-done.2 = bf16[8,256,128]{2,1,0:T(8,128)(2,1)S(1)} async-done(((bf16[8,256,128]{2,1,0:T(8,128)(2,1)}), bf16[8,256,128]{2,1,0:T(8,128)(2,1)S(1)}, u32[]{:S(2)}, u32[]{:S(2)}) %all-to-all-start.2) | async-done | bytes 524320 | tf_op jit(solution)/shard_map/all_to_all | solution.py:30
  90.8 3.4 %all-to-all-start.3 = ((bf16[8,64,256]{2,1,0:T(8,128)(2,1)}), bf16[8,64,256]{2,1,0:T(8,128)(2,1)S(1)}, u32[]{:S(2)}, u32[]{:S(2)}) async-start(bf16[8,64,256]{2,1,0:T(8,128)(2,1)} %bitcast.4), calls=%async_computation.3 | async-start | bytes 524288 | tf_op jit(solution)/shard_map/all_to_all | solution.py:30
  94.2 0.4 copy.10
  94.6 1.2 %reshape.30 = bf16[64,4096]{1,0:T(8,128)(2,1)} reshape(bf16[64,8,4,128]{3,2,1,0:T(4,128)(2,1)S(1)} %copy.10) | data formatting | bytes 1048576 | tf_op jit(solution)/shard_map/reshape | solution.py:263
  95.8 7.1 %all-to-all-done.3 = bf16[8,64,256]{2,1,0:T(8,128)(2,1)S(1)} async-done(((bf16[8,64,256]{2,1,0:T(8,128)(2,1)}), bf16[8,64,256]{2,1,0:T(8,128)(2,1)S(1)}, u32[]{:S(2)}, u32[]{:S(2)}) %all-to-all-start.3) | async-done | bytes 262176 | tf_op jit(solution)/shard_map/all_to_all | solution.py:30
  103.0 0.7 copy_bitcast_fusion
  (10 shorter events, 0.3 us)
Async XLA Ops:
  19.3 28.5 %copy-start = (s32[64]{0:T(128)S(1)}, s32[64]{0:T(128)}, u32[]{:S(2)}) copy-start(s32[64]{0:T(128)} %order_ref.1) | copy-start | bytes 772
  19.3 28.5 %copy-start.1 = (s32[64]{0:T(128)S(1)}, s32[64]{0:T(128)}, u32[]{:S(2)}) copy-start(s32[64]{0:T(128)} %start_ref.1) | copy-start | bytes 772
  19.3 28.5 %all-to-all-start = ((bf16[8,528,128]{2,1,0:T(8,128)(2,1)}), bf16[8,528,128]{2,1,0:T(8,128)(2,1)S(1)}, u32[]{:S(2)}, u32[]{:S(2)}) async-start(bf16[8,528,128]{2,1,0:T(8,128)(2,1)} %get-tuple-element.11), calls=%async_computation | async-start | bytes 2162688 | tf_op jit(solution)/shard_map/all_to_all | solution.py:30
  23.0 11.0 %collective-permute-start.3 = (bf16[512,256]{1,0:T(8,128)(2,1)S(1)}, bf16[512,256]{1,0:T(8,128)(2,1)S(1)}, u32[]{:S(2)}, u32[]{:S(2)}) collective-permute-start(bf16[512,256]{1,0:T(8,128)(2,1)S(1)} %bitcast.16), channel_id=1, source_target_pairs={{0,240},{8,248},{16,0},{24,8},{32,16},{40,24},{48,32},{56,40},{64,... | collective-permute-start | bytes 786440 | tf_op jit(solution)/shard_map/ppermute | solution.py:26
  29.8 7.0 %collective-permute-start.2 = (bf16[512,256]{1,0:T(8,128)(2,1)S(1)}, bf16[512,256]{1,0:T(8,128)(2,1)S(1)}, u32[]{:S(2)}, u32[]{:S(2)}) collective-permute-start(bf16[512,256]{1,0:T(8,128)(2,1)S(1)} %bitcast.17), channel_id=1, source_target_pairs={{0,248},{8,0},{16,8},{24,16},{32,24},{40,32},{48,40},{56,48},{64,5... | collective-permute-start | bytes 786440 | tf_op jit(solution)/shard_map/ppermute | solution.py:26
  29.8 9.7 %collective-permute-start.1 = (bf16[512,256]{1,0:T(8,128)(2,1)S(1)}, bf16[512,256]{1,0:T(8,128)(2,1)S(1)}, u32[]{:S(2)}, u32[]{:S(2)}) collective-permute-start(bf16[512,256]{1,0:T(8,128)(2,1)S(1)} %bitcast.18), channel_id=1, source_target_pairs={{0,8},{8,16},{16,24},{24,32},{32,40},{40,48},{48,56},{56,64},{64,7... | collective-permute-start | bytes 786440 | tf_op jit(solution)/shard_map/ppermute | solution.py:26
  30.3 11.4 %collective-permute-start = (bf16[512,256]{1,0:T(8,128)(2,1)S(1)}, bf16[512,256]{1,0:T(8,128)(2,1)S(1)}, u32[]{:S(2)}, u32[]{:S(2)}) collective-permute-start(bf16[512,256]{1,0:T(8,128)(2,1)S(1)} %bitcast.19), channel_id=1, source_target_pairs={{0,16},{8,24},{16,32},{24,40},{32,48},{40,56},{48,64},{56,72},{64,... | collective-permute-start | bytes 786440 | tf_op jit(solution)/shard_map/ppermute | solution.py:26
  59.6 11.0 %collective-permute-start.4 = (bf16[512,256]{1,0:T(8,128)(2,1)}, bf16[512,256]{1,0:T(8,128)(2,1)S(1)}, u32[]{:S(2)}, u32[]{:S(2)}) collective-permute-start(bf16[512,256]{1,0:T(8,128)(2,1)} %get-tuple-element.15), channel_id=1, source_target_pairs={{0,240},{8,248},{16,0},{24,8},{32,16},{40,24},{48,32},{56,40},{64,... | collective-permute-start | bytes 786440 | tf_op jit(solution)/shard_map/ppermute | solution.py:26
  66.4 7.0 %collective-permute-start.5 = (bf16[512,256]{1,0:T(8,128)(2,1)}, bf16[512,256]{1,0:T(8,128)(2,1)S(1)}, u32[]{:S(2)}, u32[]{:S(2)}) collective-permute-start(bf16[512,256]{1,0:T(8,128)(2,1)} %get-tuple-element.16), channel_id=1, source_target_pairs={{0,248},{8,0},{16,8},{24,16},{32,24},{40,32},{48,40},{56,48},{64,5... | collective-permute-start | bytes 786440 | tf_op jit(solution)/shard_map/ppermute | solution.py:26
  66.4 9.6 %collective-permute-start.6 = (bf16[512,256]{1,0:T(8,128)(2,1)S(1)}, bf16[512,256]{1,0:T(8,128)(2,1)S(1)}, u32[]{:S(2)}, u32[]{:S(2)}) collective-permute-start(bf16[512,256]{1,0:T(8,128)(2,1)S(1)} %get-tuple-element.17), channel_id=1, source_target_pairs={{0,8},{8,16},{16,24},{24,32},{32,40},{40,48},{48,56},{56,64},{64,7... | collective-permute-start | bytes 786440 | tf_op jit(solution)/shard_map/ppermute | solution.py:26
  66.9 11.3 %collective-permute-start.7 = (bf16[512,256]{1,0:T(8,128)(2,1)S(1)}, bf16[512,256]{1,0:T(8,128)(2,1)S(1)}, u32[]{:S(2)}, u32[]{:S(2)}) collective-permute-start(bf16[512,256]{1,0:T(8,128)(2,1)S(1)} %get-tuple-element.18), channel_id=1, source_target_pairs={{0,16},{8,24},{16,32},{24,40},{32,48},{40,56},{48,64},{56,72},{64,... | collective-permute-start | bytes 786440 | tf_op jit(solution)/shard_map/ppermute | solution.py:26
  66.9 23.9 %all-to-all-start.2 = ((bf16[8,256,128]{2,1,0:T(8,128)(2,1)}), bf16[8,256,128]{2,1,0:T(8,128)(2,1)S(1)}, u32[]{:S(2)}, u32[]{:S(2)}) async-start(bf16[8,256,128]{2,1,0:T(8,128)(2,1)} %get-tuple-element.13), calls=%async_computation.2 | async-start | bytes 1048576 | tf_op jit(solution)/shard_map/all_to_all | solution.py:30
  90.8 12.1 %all-to-all-start.3 = ((bf16[8,64,256]{2,1,0:T(8,128)(2,1)}), bf16[8,64,256]{2,1,0:T(8,128)(2,1)S(1)}, u32[]{:S(2)}, u32[]{:S(2)}) async-start(bf16[8,64,256]{2,1,0:T(8,128)(2,1)} %bitcast.4), calls=%async_computation.3 | async-start | bytes 524288 | tf_op jit(solution)/shard_map/all_to_all | solution.py:30
where the time goes:
time: 102 us; the launch traced here: 104 us
  waiting for transfers between devices  44.1 us (43%)
  starting transfers between devices  25.2 us (25%)
  Pallas kernels  15.6 us (15%)
  blocking collectives  14.8 us (15%)
  local copies, waits for them, and re-layouts  2.4 us (2%)
    all_to_all x3, waiting for transfers between devices, swap_heads(): lax.all_to_all(value, 'head', split_axis=0, concat_axis=0, tiled=True)  24.9 us
    ppermute x8, waiting for transfers between devices, send(): lax.ppermute(value, 'seq', [(i, (i + steps) % count) for i in range(count)])  19.2 us
    all_to_all x1, blocking collectives, swap_heads(): lax.all_to_all(value, 'head', split_axis=0, concat_axis=0, tiled=True)  14.8 us
    ppermute x8, starting transfers between devices, send(): lax.ppermute(value, 'seq', [(i, (i + steps) % count) for i in range(count)])  14.6 us
    pallas_call x1, Pallas kernels, attention(): pl.pallas_call(functools.partial(attention_kernel, seq_size), in_specs=[s...  11.8 us
    all_to_all x3, starting transfers between devices, swap_heads(): lax.all_to_all(value, 'head', split_axis=0, concat_axis=0, tiled=True)  10.6 us
    pallas_call x1, Pallas kernels, pack(): pl.pallas_call(functools.partial(pack_kernel, owners), grid=(heads // own...  3.86 us
  transfers between devices with their start and end apart: 11, of which 11 were waited for; matrix products, arithmetic and copies ran while one was open for 2% of the time, Pallas kernels for 0%

commit v1 on v0

v1 whole, which is shorter than its diff:
```python
import functools
import math

import jax
import jax.numpy as jnp
from jax import lax
from jax.experimental import pallas as pl
from jax.experimental.pallas import tpu as pltpu
from jax.sharding import PartitionSpec as P

QUERY_HEADS = 32
KEY_VALUE_HEADS = 8
GROUP = QUERY_HEADS // KEY_VALUE_HEADS
HEAD = 128
REACH = 2
BLK = 256
SCALE = 1.0 / math.sqrt(HEAD)
SCALE2 = SCALE * math.log2(math.e)
MASKED = -1e30
DELTA_ROWS = 16
MIB = 1024 * 1024
NEAR = 4
BLOCKS = 10


def send(value, steps):
    count = lax.axis_size("seq")
    return lax.ppermute(value, "seq", [(i, (i + steps) % count) for i in range(count)])


def swap_pair(value):
    count = lax.axis_size("seq")
    return lax.ppermute(value, "seq", [(i, i ^ 1) for i in range(count)])


def swap_cross(value):
    count = lax.axis_size("seq")
    return lax.ppermute(value, "seq", [(i, (i + (1 if i % 2 else count - 1)) % count) for i in range(count)])


def swap_heads(value):
    return lax.all_to_all(value, "head", split_axis=0, concat_axis=0, tiled=True)


def near_array(shape, dtype):
    return pltpu.VMEM(shape, dtype)


def near(value):
    return pltpu.with_memory_space_constraint(value, pltpu.VMEM)


SMEM = pl.BlockSpec(memory_space=pltpu.SMEM)
VMEM = pl.BlockSpec(memory_space=pltpu.VMEM)


def pack_kernel(owners, q_ref, g_ref, o_ref, k_ref, v_ref, out_ref):
    rows = q_ref.shape[0]
    width = GROUP * HEAD
    base = 2 * GROUP * rows
    for n in range(owners):
        deltas = []
        for h in range(GROUP):
            cols = slice(n * width + h * HEAD, n * width + (h + 1) * HEAD)
            grad = g_ref[:, cols]
            out_ref[n, h * rows : (h + 1) * rows, :] = q_ref[:, cols]
            out_ref[n, (GROUP + h) * rows : (GROUP + h + 1) * rows, :] = grad
            deltas.append(grad.astype(jnp.float32) * o_ref[:, cols].astype(jnp.float32))
        lines = []
        for h in range(0, GROUP, 2):
            both = jnp.concatenate(deltas[h : h + 2], axis=0)
            lines.append(jnp.sum(both.T, axis=0, keepdims=True))
        delta = jnp.concatenate(lines, axis=0)
        high = delta.astype(jnp.bfloat16).astype(jnp.float32)
        spare = jnp.zeros((DELTA_ROWS - GROUP, HEAD), jnp.float32)
        tile = jnp.concatenate([high, delta - high, spare], axis=0)
        out_ref[n, base : base + DELTA_ROWS, :] = tile.astype(jnp.bfloat16)
        out_ref[n, base + DELTA_ROWS : base + DELTA_ROWS + rows, :] = k_ref[:, n * HEAD : (n + 1) * HEAD]
        out_ref[n, base + DELTA_ROWS + rows :, :] = v_ref[:, n * HEAD : (n + 1) * HEAD]


def pack(queries, keys, values, grads, outputs, heads):
    rows = queries.shape[0]
    owners = 2
    wide = pl.BlockSpec((rows, owners * GROUP * HEAD), lambda n: (0, n))
    narrow = pl.BlockSpec((rows, owners * HEAD), lambda n: (0, n))
    out_rows = (2 * GROUP + 2) * rows + DELTA_ROWS
    return pl.pallas_call(
        functools.partial(pack_kernel, owners),
        grid=(heads // owners,),
        in_specs=[wide, wide, wide, narrow, narrow],
        out_specs=pl.BlockSpec((owners, out_rows, HEAD), lambda n: (n, 0, 0)),
        out_shape=jax.ShapeDtypeStruct((heads, out_rows, HEAD), jnp.bfloat16),
        name="pack",
    )(queries, grads, outputs, keys, values)


def plan_kernel(seq_size, mine_ref, order_ref, start_ref, keep_ref, docs_ref):
    def count(b, running):
        running = running + jnp.where(b > 0, start_ref[b], 0)
        docs_ref[b] = running
        return running

    lax.fori_loop(0, order_ref.shape[0], count, jnp.int32(0))
    mine = mine_ref[0]
    odd = lax.rem(mine, 2)
    steps = (0, 1 - 2 * odd, -REACH, REACH, 2 * odd - 1)
    blocks = []
    for step in steps:
        slab = lax.rem(mine + step + seq_size, seq_size)
        blocks += [order_ref[2 * slab], order_ref[2 * slab + 1]]
    docs = [docs_ref[b] for b in blocks]
    for i in range(2):
        for j in range(BLOCKS):
            kept = (blocks[j] <= blocks[i]) & (docs[j] == docs[i])
            keep_ref[i * BLOCKS + j] = kept.astype(jnp.int32)


def plan(mine, block_order, doc_start, seq_size):
    return pl.pallas_call(
        functools.partial(plan_kernel, seq_size),
        in_specs=[SMEM] * 3,
        out_specs=SMEM,
        out_shape=jax.ShapeDtypeStruct((2 * BLOCKS,), jnp.int32),
        scratch_shapes=[pltpu.SMEM((block_order.shape[0],), jnp.int32)],
        name="plan",
    )(mine, block_order, doc_start)


def block_of(ref, j, first, rows):
    per_block = BLK // rows
    tiles = ref[pl.ds(j * per_block, per_block), first : first + rows, :]
    return tiles.reshape(BLK, HEAD)


def near_kernel(rows, keep_ref, got_ref, pair_ref, e_ref, d_ref, qt_ref, gt_ref, u_ref, stat_ref, kv, scores):
    per_block = BLK // rows
    chunk = GROUP * rows
    sources = 2 * per_block
    kv_at = 2 * chunk + DELTA_ROWS
    kv[:sources] = got_ref[:, kv_at:, :]
    kv[sources:] = pair_ref[...]

    def score(i, j, diagonal):
        keys = block_of(kv, j, 0, rows)
        for c in range(per_block):
            lanes = slice(c * chunk, (c + 1) * chunk)
            s = jnp.dot(keys, qt_ref[i, :, lanes], preferred_element_type=jnp.float32)
            if diagonal:
                key_at = lax.broadcasted_iota(jnp.int32, (BLK, chunk), 0)
                query_at = c * rows + lax.broadcasted_iota(jnp.int32, (BLK, chunk), 1) % rows
                s = jnp.where(key_at <= query_at, s, MASKED)
            scores[j, :, lanes] = s
            top = jnp.max(s, axis=0, keepdims=True)
            stat_ref[i, 0:1, lanes] = top if diagonal else jnp.maximum(top, stat_ref[i, 0:1, lanes])

    def weigh(i, j, first):
        keys_t = block_of(kv, j, 0, rows).T
        values = block_of(kv, j, rows, rows)
        parts = []
        for c in range(per_block):
            lanes = slice(c * chunk, (c + 1) * chunk)
            e = jnp.exp2((scores[j, :, lanes] - stat_ref[i, 0:1, lanes]) * SCALE2)
            total = jnp.sum(e, axis=0, keepdims=True)
            stat_ref[i, 1:2, lanes] = total if first else stat_ref[i, 1:2, lanes] + total
            dprobs = jnp.dot(values, gt_ref[i, :, lanes], preferred_element_type=jnp.float32)
            d = (e * (dprobs - stat_ref[i, 2:3, lanes])).astype(jnp.bfloat16)
            e_ref[i * NEAR + j, :, lanes] = e.astype(jnp.bfloat16)
            d_ref[i * NEAR + j, :, lanes] = d
            parts.append(d)
        u = jnp.dot(keys_t, jnp.concatenate(parts, axis=1), preferred_element_type=jnp.float32)
        u_ref[i] = u if first else u_ref[i] + u

    for i in range(2):
        for c in range(per_block):
            source = i * per_block + c
            lanes = slice(c * chunk, (c + 1) * chunk)
            qt_ref[i, :, lanes] = got_ref[source, :chunk, :].T
            gt_ref[i, :, lanes] = got_ref[source, chunk : 2 * chunk, :].T
            tile = got_ref[source, 2 * chunk : kv_at, :].astype(jnp.float32)
            delta = tile[0:2, :] + tile[2:4, :]
            stat_ref[i, 2:3, c * chunk : c * chunk + HEAD] = delta[0:1, :]
            stat_ref[i, 2:3, c * chunk + HEAD : (c + 1) * chunk] = delta[1:2, :]
        score(i, i, True)

        def visit_scores(j, _):
            @pl.when((keep_ref[i * BLOCKS + j] == 1) & (j != i))
            def _():
                score(i, j, False)

            return 0

        lax.fori_loop(0, NEAR, visit_scores, 0)
        weigh(i, i, True)

        def visit_weights(j, _):
            @pl.when((keep_ref[i * BLOCKS + j] == 1) & (j != i))
            def _():
                weigh(i, j, False)

            return 0

        lax.fori_loop(0, NEAR, visit_weights, 0)


def near_part(keep, got, pair, rows):
    lanes = BLK * GROUP
    return pl.pallas_call(
        functools.partial(near_kernel, rows),
        in_specs=[SMEM, VMEM, VMEM],
        out_specs=[VMEM] * 6,
        out_shape=[
            near_array((2 * NEAR, BLK, lanes), jnp.bfloat16),
            near_array((2 * NEAR, BLK, lanes), jnp.bfloat16),
            near_array((2, HEAD, lanes), jnp.bfloat16),
            near_array((2, HEAD, lanes), jnp.bfloat16),
            near_array((2, HEAD, lanes), jnp.float32),
            near_array((2, 8, lanes), jnp.float32),
        ],
        scratch_shapes=[
            pltpu.VMEM((2 * pair.shape[0],) + pair.shape[1:], jnp.bfloat16),
            pltpu.VMEM((NEAR, BLK, lanes), jnp.float32),
        ],
        compiler_params=pltpu.CompilerParams(vmem_limit_bytes=24 * MIB),
        cost_estimate=pl.CostEstimate(flops=3_000_000_000, bytes_accessed=4_000_000, transcendentals=8_000_000),
        name="near_part",
    )(keep, got, pair)


def far_kernel(
    rows, keep_ref, got_ref, before_ref, after_ref, cross_ref, e_ref, d_ref, qt_ref, gt_ref, u_ref,
    stat_ref, to_before, to_after, to_cross, to_pair, out_ref, own_ref, kv, scores, acc, stats, dqt_ref, alpha_ref,
):
    per_block = BLK // rows
    chunk = GROUP * rows
    sources = 2 * per_block
    far_blocks = BLOCKS - NEAR
    kv[:sources] = before_ref[...]
    kv[sources : 2 * sources] = after_ref[...]

    kv[2 * sources :] = cross_ref[...]
    acc[...] = jnp.zeros_like(acc)

    def score(i, j):
        keys = block_of(kv, j, 0, rows)
        for c in range(per_block):
            lanes = slice(c * chunk, (c + 1) * chunk)
            s = jnp.dot(keys, qt_ref[i, :, lanes], preferred_element_type=jnp.float32)
            scores[j, :, lanes] = s
            before = stats[0:1, lanes]
            top = jnp.maximum(jnp.max(s, axis=0, keepdims=True), before)
            stats[0:1, lanes] = top
            stats[1:2, lanes] = stats[1:2, lanes] * jnp.exp2((before - top) * SCALE2) + jnp.sum(
                jnp.exp2((s - top) * SCALE2), axis=0, keepdims=True
            )

    def queries_of(i, first):
        tiles = got_ref[i * per_block : (i + 1) * per_block, first : first + chunk, :]
        return tiles.reshape(per_block * chunk, HEAD)

    def add(j, k, v):
        here = pl.ds(j * per_block, per_block)
        acc[here, :rows, :] += k.reshape(per_block, rows, HEAD)
        acc[here, rows:, :] += v.reshape(per_block, rows, HEAD)

    def gradients(i, j):
        keys_t = block_of(kv, j, 0, rows).T
        values = block_of(kv, j, rows, rows)
        all_p, all_d = [], []
        for c in range(per_block):
            lanes = slice(c * chunk, (c + 1) * chunk)
            probs = jnp.exp2(scores[j, :, lanes] * SCALE2 - stats[2:3, lanes])
            dprobs = jnp.dot(values, gt_ref[i, :, lanes], preferred_element_type=jnp.float32)
            all_d.append(((SCALE * probs) * (dprobs - stat_ref[i, 2:3, lanes])).astype(jnp.bfloat16))
            all_p.append(probs.astype(jnp.bfloat16))
        probs = jnp.concatenate(all_p, axis=1)
        dscores = jnp.concatenate(all_d, axis=1)
        v = jnp.dot(probs, queries_of(i, chunk), preferred_element_type=jnp.float32)
        k = jnp.dot(dscores, queries_of(i, 0), preferred_element_type=jnp.float32)
        dqt_ref[i] += jnp.dot(keys_t, dscores, preferred_element_type=jnp.float32)
        add(j, k, v)

    def pair_gradients(i, j):
        p = (e_ref[i * NEAR + j].astype(jnp.float32) * alpha_ref[i, 0:1, :]).astype(jnp.bfloat16)
        d = (d_ref[i * NEAR + j].astype(jnp.float32) * alpha_ref[i, 1:2, :]).astype(jnp.bfloat16)
        v = jnp.dot(p, queries_of(i, chunk), preferred_element_type=jnp.float32)
        k = jnp.dot(d, queries_of(i, 0), preferred_element_type=jnp.float32)
        add(far_blocks + j, k, v)

    for i in range(2):
        stats[0:2, :] = stat_ref[i, 0:2, :]

        def visit_scores(j, _):
            @pl.when(keep_ref[i * BLOCKS + NEAR + j] == 1)
            def _():
                score(i, j)

            return 0

        lax.fori_loop(0, far_blocks, visit_scores, 0)
        lse = stats[0:1, :] * SCALE2 + jnp.log2(stats[1:2, :])
        stats[2:3, :] = lse
        alpha = jnp.exp2(stat_ref[i, 0:1, :] * SCALE2 - lse)
        alpha_ref[i, 0:1, :] = alpha
        alpha_ref[i, 1:2, :] = alpha * SCALE
        dqt_ref[i] = u_ref[i] * (alpha * SCALE)

        def visit_gradients(j, _):
            @pl.when(keep_ref[i * BLOCKS + NEAR + j] == 1)
            def _():
                gradients(i, j)

            return 0

        lax.fori_loop(0, far_blocks, visit_gradients, 0)

        def visit_pair(j, _):
            @pl.when(keep_ref[i * BLOCKS + j] == 1)
            def _():
                pair_gradients(i, j)

            return 0

        lax.fori_loop(0, NEAR, visit_pair, 0)
        for c in range(per_block):
            dq = dqt_ref[i, :, c * chunk : (c + 1) * chunk].T
            out_ref[i * per_block + c, :chunk, :] = dq.astype(jnp.bfloat16)

    own_ref[...] = acc[3 * sources : 4 * sources]
    for n, ref in enumerate((to_before, to_after, to_cross)):
        ref[...] = acc[n * sources : (n + 1) * sources].astype(jnp.bfloat16)
    to_pair[...] = acc[4 * sources :].astype(jnp.bfloat16)


def far_part(keep, got, before, after, cross, state, rows):
    lanes = BLK * GROUP
    e, d, qt, gt, u, stat = state
    chunk = GROUP * rows
    sources, tall, _ = before.shape
    return pl.pallas_call(
        functools.partial(far_kernel, rows),
        in_specs=[SMEM] + [VMEM] * 10,
        out_specs=[VMEM] * 6,
        out_shape=[
            *[jax.ShapeDtypeStruct((sources, tall, HEAD), jnp.bfloat16)] * 4,
            jax.ShapeDtypeStruct((sources, chunk + tall, HEAD), jnp.bfloat16),
            jax.ShapeDtypeStruct((sources, tall, HEAD), jnp.float32),
        ],
        scratch_shapes=[
            pltpu.VMEM((3 * sources, tall, HEAD), jnp.bfloat16),
            pltpu.VMEM((BLOCKS - NEAR, BLK, lanes), jnp.float32),
            pltpu.VMEM((5 * sources, tall, HEAD), jnp.float32),
            pltpu.VMEM((8, lanes), jnp.float32),
            pltpu.VMEM((2, HEAD, lanes), jnp.float32),
            pltpu.VMEM((2, 8, lanes), jnp.float32),
        ],
        compiler_params=pltpu.CompilerParams(vmem_limit_bytes=24 * MIB),
        cost_estimate=pl.CostEstimate(flops=3_000_000_000, bytes_accessed=4_000_000, transcendentals=8_000_000),
        name="far_part",
    )(keep, got, before, after, cross, e, d, qt, gt, u, stat)


def unpack_kernel(rows, got_ref, q_ref, k_ref, v_ref):
    width = GROUP * HEAD
    for n in range(got_ref.shape[0]):
        for h in range(GROUP):
            q_ref[:, n * width + h * HEAD : n * width + (h + 1) * HEAD] = got_ref[n, h * rows : (h + 1) * rows, :]
        k_ref[:, n * HEAD : (n + 1) * HEAD] = got_ref[n, GROUP * rows : (GROUP + 1) * rows, :]
        v_ref[:, n * HEAD : (n + 1) * HEAD] = got_ref[n, (GROUP + 1) * rows :, :]


def unpack(got, rows):
    heads = got.shape[0]
    owners = 4
    return pl.pallas_call(
        functools.partial(unpack_kernel, rows),
        grid=(heads // owners,),
        in_specs=[pl.BlockSpec((owners,) + got.shape[1:], lambda n: (n, 0, 0))],
        out_specs=[
            pl.BlockSpec((rows, owners * GROUP * HEAD), lambda n: (0, n)),
            pl.BlockSpec((rows, owners * HEAD), lambda n: (0, n)),
            pl.BlockSpec((rows, owners * HEAD), lambda n: (0, n)),
        ],
        out_shape=[
            jax.ShapeDtypeStruct((rows, heads * GROUP * HEAD), jnp.bfloat16),
            jax.ShapeDtypeStruct((rows, heads * HEAD), jnp.bfloat16),
            jax.ShapeDtypeStruct((rows, heads * HEAD), jnp.bfloat16),
        ],
        name="unpack",
    )(got)


def local(queries, keys, values, output_gradient, outputs, block_order, doc_start):
    heads = lax.axis_size("head")
    seq_size = lax.axis_size("seq")
    rows = queries.shape[0]
    place = lax.axis_index("seq").astype(jnp.int32)
    keep = plan(place.reshape(1), block_order, doc_start, seq_size)
    got = swap_heads(pack(queries, keys, values, output_gradient, outputs, heads))
    kv = got[:, 2 * GROUP * rows + DELTA_ROWS :, :]
    kv, keep = lax.optimization_barrier((kv, keep))
    pair = swap_pair(kv)
    before, after, cross = send(kv, REACH), send(kv, -REACH), swap_cross(kv)
    state = near_part(keep, near(got), near(pair), rows)
    before, after, cross, *state = lax.optimization_barrier((before, after, cross, *state))
    *sums, out, own = far_part(
        keep, near(got), near(before), near(after), near(cross), [near(x) for x in state], rows
    )
    to_before, to_after, to_cross, to_pair = sums
    back = (send(to_before, -REACH), send(to_after, REACH), swap_cross(to_cross), swap_pair(to_pair))
    total = own
    for part in back:
        total = total + part.astype(jnp.float32)
    out = lax.dynamic_update_slice(out, total.astype(jnp.bfloat16), (0, GROUP * rows, 0))
    return tuple(unpack(swap_heads(out), rows))


def solution(mesh):
    rows = P(("seq", "head"), None)
    return jax.shard_map(
        local,
        mesh=mesh,
        in_specs=(rows, rows, rows, rows, rows, P(), P()),
        out_specs=(rows, rows, rows),
        check_vma=False,
    )
```

time: 102 us -> 85.8 us (0.84); the launches traced: 104 us -> 85.5 us
  waiting for transfers between devices: 44.1 us -> 32.8 us
  starting transfers between devices: 25.2 us -> 20.4 us
  local copies, waits for them, and re-layouts: 2.4 us -> 0.67 us
    ppermute x8 -> x4, starting transfers between devices: 14.6 us -> 6.35 us  [send(): lax.ppermute(value, 'seq', [(i, (i + steps) % count) for i in range(count)])]
    ppermute x0 -> x4, starting transfers between devices: none -> 8.05 us  [the longest x2 7.95 us: swap_cross(): lax.ppermute(value, 'seq', [(i, (i + (1 if i % 2 else count - 1)) % count...]
    all_to_all x3 -> x1, waiting for transfers between devices: 24.9 us -> 18.8 us  [swap_heads(): lax.all_to_all(value, 'head', split_axis=0, concat_axis=0, tiled=True)]
    ppermute x8 -> x4, waiting for transfers between devices: 19.2 us -> 14 us  [send(): lax.ppermute(value, 'seq', [(i, (i + steps) % count) for i in range(count)])]
    all_to_all x3 -> x1, starting transfers between devices: 10.6 us -> 6.03 us  [swap_heads(): lax.all_to_all(value, 'head', split_axis=0, concat_axis=0, tiled=True)]
    reshape x2 -> x0, local copies, waits for them, and re-layouts: 1.92 us -> none  [the longest x1 1.18 us: local(): dq.reshape(heads, GROUP, rows, HEAD).transpose(2, 0, 1, 3)]
    pallas_call x1 -> x4, Pallas kernels: 11.8 us -> 12.1 us  [the longest x1 5.16 us: far_part(): pl.pallas_call(functools.partial(far_kernel, rows), in_specs=[SMEM] + [VM...]
  transfers between devices with their start and end apart: 11 -> 9, of which waited for: 11 -> 6; matrix products, arithmetic and copies ran while one was open for 2% -> 0% of each run, Pallas kernels for 0% -> 6%
where the time goes in v1:
time: 85.8 us; the launch traced here: 85.5 us
  waiting for transfers between devices  32.8 us (38%)
  starting transfers between devices  20.4 us (24%)
  Pallas kernels  16 us (19%)
  blocking collectives  14.7 us (17%)
    all_to_all x1, waiting for transfers between devices, swap_heads(): lax.all_to_all(value, 'head', split_axis=0, concat_axis=0, tiled=True)  18.8 us
    all_to_all x1, blocking collectives, swap_heads(): lax.all_to_all(value, 'head', split_axis=0, concat_axis=0, tiled=True)  14.7 us
    ppermute x4, waiting for transfers between devices, send(): lax.ppermute(value, 'seq', [(i, (i + steps) % count) for i in range(count)])  14 us
    ppermute x2, starting transfers between devices, swap_cross(): lax.ppermute(value, 'seq', [(i, (i + (1 if i % 2 else count - 1)) % count...  7.95 us
    ppermute x4, starting transfers between devices, send(): lax.ppermute(value, 'seq', [(i, (i + steps) % count) for i in range(count)])  6.35 us
    all_to_all x1, starting transfers between devices, swap_heads(): lax.all_to_all(value, 'head', split_axis=0, concat_axis=0, tiled=True)  6.03 us
    pallas_call x1, Pallas kernels, far_part(): pl.pallas_call(functools.partial(far_kernel, rows), in_specs=[SMEM] + [VM...  5.16 us
    pallas_call x1, Pallas kernels, pack(): pl.pallas_call(functools.partial(pack_kernel, owners), grid=(heads // own...  3.93 us
  transfers between devices with their start and end apart: 9, of which 6 were waited for; matrix products, arithmetic and copies ran while one was open for 0% of the time, Pallas kernels for 6%

profile of v1, /device:TPU:2, one launch (start us, length us, event | category | flops | bytes accessed | tf_op | source)
XLA Modules:
  0.0 85.5 jit_solution(10435016624615073824)
XLA Ops:
  0.6 3.9 %pack.1 = bf16[8,656,128]{2,1,0:T(8,128)(2,1)} custom-call(bf16[64,4096]{1,0:T(8,128)(2,1)} %q_ref.1, bf16[64,4096]{1,0:T(8,128)(2,1)} %g_ref.1, bf16[64,4096]{1,0:T(8,128)(2,1)} %o_ref.1, bf16[64,1024]{1,0:T(8,128)(2,1)} %k_ref.1, bf16[64,1024]{1,0:T(8,128)(2,1)} %v_ref.1), custom_call_target="tpu_custom_call" | custom-call | tf_op jit(solution)/shard_map/pack/pallas_call | solution.py:88
  4.6 6.0 %all-to-all-start = ((bf16[8,656,128]{2,1,0:T(8,128)(2,1)}), bf16[8,656,128]{2,1,0:T(8,128)(2,1)S(1)}, u32[]{:S(2)}, u32[]{:S(2)}) async-start(bf16[8,656,128]{2,1,0:T(8,128)(2,1)} %pack.1), calls=%async_computation | async-start | bytes 2686976 | tf_op jit(solution)/shard_map/all_to_all | solution.py:42
  10.6 1.6 %plan.1.keep_ref = s32[20]{0:T(128)} custom-call(s32[1]{0:T(128)} %bitcast.mine_ref, s32[64]{0:T(128)} %order_ref.1, s32[64]{0:T(128)} %start_ref.1), custom_call_target="tpu_custom_call" | custom-call | tf_op jit(solution)/shard_map/plan/pallas_call | solution.py:120
  12.2 18.8 %all-to-all-done.got_ref = bf16[8,656,128]{2,1,0:T(8,128)(2,1)S(1)} async-done(((bf16[8,656,128]{2,1,0:T(8,128)(2,1)}), bf16[8,656,128]{2,1,0:T(8,128)(2,1)S(1)}, u32[]{:S(2)}, u32[]{:S(2)}) %all-to-all-start) | async-done | bytes 1343520 | tf_op jit(solution)/shard_map/all_to_all | solution.py:42
  31.0 0.1 collective-permute-start.3
  31.1 6.8 %collective-permute-start.2 = (bf16[8,128,128]{2,1,0:T(8,128)(2,1)S(1)}, bf16[8,128,128]{2,1,0:T(8,128)(2,1)S(1)}, u32[]{:S(2)}, u32[]{:S(2)}) collective-permute-start(bf16[8,128,128]{2,1,0:T(8,128)(2,1)S(1)} %slice.4), channel_id=1, source_target_pairs={{0,248},{8,16},{16,8},{24,32},{32,24},{40,48},{48,40},{56,64},{64,... | collective-permute-start | bytes 786440 | tf_op jit(solution)/shard_map/ppermute | solution.py:38
  37.9 1.0 %collective-permute-start.1 = (bf16[8,128,128]{2,1,0:T(8,128)(2,1)S(1)}, bf16[8,128,128]{2,1,0:T(8,128)(2,1)S(1)}, u32[]{:S(2)}, u32[]{:S(2)}) collective-permute-start(bf16[8,128,128]{2,1,0:T(8,128)(2,1)S(1)} %slice.4), channel_id=1, source_target_pairs={{0,240},{8,248},{16,0},{24,8},{32,16},{40,24},{48,32},{56,40},{64,... | collective-permute-start | bytes 786440 | tf_op jit(solution)/shard_map/ppermute | solution.py:28
  39.0 1.0 %collective-permute-start = (bf16[8,128,128]{2,1,0:T(8,128)(2,1)S(1)}, bf16[8,128,128]{2,1,0:T(8,128)(2,1)S(1)}, u32[]{:S(2)}, u32[]{:S(2)}) collective-permute-start(bf16[8,128,128]{2,1,0:T(8,128)(2,1)S(1)} %slice.4), channel_id=1, source_target_pairs={{0,16},{8,24},{16,32},{24,40},{32,48},{40,56},{48,64},{56,72},{64,... | collective-permute-start | bytes 786440 | tf_op jit(solution)/shard_map/ppermute | solution.py:28
  40.0 0.7 copy-done
  40.6 3.4 %near_part.1 = (bf16[8,256,1024]{2,1,0:T(8,128)(2,1)S(1)}, bf16[8,256,1024]{2,1,0:T(8,128)(2,1)S(1)}, bf16[2,128,1024]{2,1,0:T(8,128)(2,1)S(1)}, bf16[2,128,1024...) custom-call(s32[20]{0:T(128)S(1)} %copy-done, ...), custom_call_target="tpu_custom_call" | custom-call | flops 3000000000 | bytes 4000000 | tf_op jit(solution)/shard_map/near_part/pallas_call | solution.py:208
  44.0 0.1 collective-permute-done.2.cross_ref
  44.1 2.8 %collective-permute-done.1.after_ref = bf16[8,128,128]{2,1,0:T(8,128)(2,1)S(1)} collective-permute-done((bf16[8,128,128]{2,1,0:T(8,128)(2,1)S(1)}, bf16[8,128,128]{2,1,0:T(8,128)(2,1)S(1)}, u32[]{:S(2)}, u32[]{:S(2)}) %collective-permute-start.1) | collective-permute-done | bytes 262176 | tf_op jit(solution)/shard_map/ppermute | solution.py:28
  46.9 1.5 %collective-permute-done.before_ref = bf16[8,128,128]{2,1,0:T(8,128)(2,1)S(1)} collective-permute-done((bf16[8,128,128]{2,1,0:T(8,128)(2,1)S(1)}, bf16[8,128,128]{2,1,0:T(8,128)(2,1)S(1)}, u32[]{:S(2)}, u32[]{:S(2)}) %collective-permute-start) | collective-permute-done | bytes 262176 | tf_op jit(solution)/shard_map/ppermute | solution.py:28
  48.4 5.2 %far_part.1 = (bf16[8,128,128]{2,1,0:T(8,128)(2,1)S(1)}, bf16[8,128,128]{2,1,0:T(8,128)(2,1)S(1)}, bf16[8,128,128]{2,1,0:T(8,128)(2,1)S(1)}, bf16[8,128,128]{2,1...) custom-call(s32[20]{0:T(128)S(1)} %copy-done, ...), custom_call_target="tpu_custom_call" | custom-call | flops 3000000000 | bytes 4000000 | tf_op jit(solution)/shard_map/far_part/pallas_call | solution.py:340
  53.6 4.3 %collective-permute-start.4 = (bf16[8,128,128]{2,1,0:T(8,128)(2,1)S(1)}, bf16[8,128,128]{2,1,0:T(8,128)(2,1)S(1)}, u32[]{:S(2)}, u32[]{:S(2)}) collective-permute-start(bf16[8,128,128]{2,1,0:T(8,128)(2,1)S(1)} %get-tuple-element.45), channel_id=1, source_target_pairs={{0,240},{8,248},{16,0},{24,8},{32,16},{40,24},{48,32},{56,40},{64,... | collective-permute-start | bytes 786440 | tf_op jit(solution)/shard_map/ppermute | solution.py:28
  57.9 0.0 collective-permute-start.5
  57.9 1.1 %collective-permute-start.6 = (bf16[8,128,128]{2,1,0:T(8,128)(2,1)S(1)}, bf16[8,128,128]{2,1,0:T(8,128)(2,1)S(1)}, u32[]{:S(2)}, u32[]{:S(2)}) collective-permute-start(bf16[8,128,128]{2,1,0:T(8,128)(2,1)S(1)} %get-tuple-element.47), channel_id=1, source_target_pairs={{0,248},{8,16},{16,8},{24,32},{32,24},{40,48},{48,40},{56,64},{64,... | collective-permute-start | bytes 786440 | tf_op jit(solution)/shard_map/ppermute | solution.py:38
  59.0 0.0 collective-permute-start.7
  59.0 2.8 %collective-permute-done.4 = bf16[8,128,128]{2,1,0:T(8,128)(2,1)S(1)} collective-permute-done((bf16[8,128,128]{2,1,0:T(8,128)(2,1)S(1)}, bf16[8,128,128]{2,1,0:T(8,128)(2,1)S(1)}, u32[]{:S(2)}, u32[]{:S(2)}) %collective-permute-start.4) | collective-permute-done | bytes 262176 | tf_op jit(solution)/shard_map/ppermute | solution.py:28
  61.8 6.9 %collective-permute-done.5 = bf16[8,128,128]{2,1,0:T(8,128)(2,1)S(1)} collective-permute-done((bf16[8,128,128]{2,1,0:T(8,128)(2,1)S(1)}, bf16[8,128,128]{2,1,0:T(8,128)(2,1)S(1)}, u32[]{:S(2)}, u32[]{:S(2)}) %collective-permute-start.5) | collective-permute-done | bytes 262176 | tf_op jit(solution)/shard_map/ppermute | solution.py:28
  68.7 0.0 collective-permute-done.6
  68.7 0.2 fusion
  68.9 14.7 %all_to_all.10.got_ref = bf16[8,384,128]{2,1,0:T(8,128)(2,1)} all-to-all(bf16[8,384,128]{2,1,0:T(8,128)(2,1)S(1)} %fusion), channel_id=1, replica_groups=mesh['seq'=32,'head'=8] {'head'}, dimensions={0} | all-to-all | bytes 1572864 | tf_op jit(solution)/shard_map/all_to_all | solution.py:42
  83.6 1.9 %unpack.1 = (bf16[64,4096]{1,0:T(8,128)(2,1)}, bf16[64,1024]{1,0:T(8,128)(2,1)}, bf16[64,1024]{1,0:T(8,128)(2,1)}) custom-call(bf16[8,384,128]{2,1,0:T(8,128)(2,1)} %all_to_all.10.got_ref), custom_call_target="tpu_custom_call" | custom-call | tf_op jit(solution)/shard_map/unpack/pallas_call | solution.py:375
  (4 shorter events, 0.0 us)
Async XLA Ops:
  4.6 26.4 %all-to-all-start = ((bf16[8,656,128]{2,1,0:T(8,128)(2,1)}), bf16[8,656,128]{2,1,0:T(8,128)(2,1)S(1)}, u32[]{:S(2)}, u32[]{:S(2)}) async-start(bf16[8,656,128]{2,1,0:T(8,128)(2,1)} %pack.1), calls=%async_computation | async-start | bytes 2686976 | tf_op jit(solution)/shard_map/all_to_all | solution.py:42
  31.0 9.0 %collective-permute-start.3 = (bf16[8,128,128]{2,1,0:T(8,128)(2,1)S(1)}, bf16[8,128,128]{2,1,0:T(8,128)(2,1)S(1)}, u32[]{:S(2)}, u32[]{:S(2)}) collective-permute-start(bf16[8,128,128]{2,1,0:T(8,128)(2,1)S(1)} %slice.4), channel_id=1, source_target_pairs={{0,8},{8,0},{16,24},{24,16},{32,40},{40,32},{48,56},{56,48},{64,72... | collective-permute-start | bytes 786440 | tf_op jit(solution)/shard_map/ppermute | solution.py:33
  31.1 13.0 %collective-permute-start.2 = (bf16[8,128,128]{2,1,0:T(8,128)(2,1)S(1)}, bf16[8,128,128]{2,1,0:T(8,128)(2,1)S(1)}, u32[]{:S(2)}, u32[]{:S(2)}) collective-permute-start(bf16[8,128,128]{2,1,0:T(8,128)(2,1)S(1)} %slice.4), channel_id=1, source_target_pairs={{0,248},{8,16},{16,8},{24,32},{32,24},{40,48},{48,40},{56,64},{64,... | collective-permute-start | bytes 786440 | tf_op jit(solution)/shard_map/ppermute | solution.py:38
  37.9 9.0 %collective-permute-start.1 = (bf16[8,128,128]{2,1,0:T(8,128)(2,1)S(1)}, bf16[8,128,128]{2,1,0:T(8,128)(2,1)S(1)}, u32[]{:S(2)}, u32[]{:S(2)}) collective-permute-start(bf16[8,128,128]{2,1,0:T(8,128)(2,1)S(1)} %slice.4), channel_id=1, source_target_pairs={{0,240},{8,248},{16,0},{24,8},{32,16},{40,24},{48,32},{56,40},{64,... | collective-permute-start | bytes 786440 | tf_op jit(solution)/shard_map/ppermute | solution.py:28
  39.0 9.5 %collective-permute-start = (bf16[8,128,128]{2,1,0:T(8,128)(2,1)S(1)}, bf16[8,128,128]{2,1,0:T(8,128)(2,1)S(1)}, u32[]{:S(2)}, u32[]{:S(2)}) collective-permute-start(bf16[8,128,128]{2,1,0:T(8,128)(2,1)S(1)} %slice.4), channel_id=1, source_target_pairs={{0,16},{8,24},{16,32},{24,40},{32,48},{40,56},{48,64},{56,72},{64,... | collective-permute-start | bytes 786440 | tf_op jit(solution)/shard_map/ppermute | solution.py:28
  40.0 0.7 copy-start
  53.6 8.2 %collective-permute-start.4 = (bf16[8,128,128]{2,1,0:T(8,128)(2,1)S(1)}, bf16[8,128,128]{2,1,0:T(8,128)(2,1)S(1)}, u32[]{:S(2)}, u32[]{:S(2)}) collective-permute-start(bf16[8,128,128]{2,1,0:T(8,128)(2,1)S(1)} %get-tuple-element.45), channel_id=1, source_target_pairs={{0,240},{8,248},{16,0},{24,8},{32,16},{40,24},{48,32},{56,40},{64,... | collective-permute-start | bytes 786440 | tf_op jit(solution)/shard_map/ppermute | solution.py:28
  57.9 10.8 %collective-permute-start.5 = (bf16[8,128,128]{2,1,0:T(8,128)(2,1)S(1)}, bf16[8,128,128]{2,1,0:T(8,128)(2,1)S(1)}, u32[]{:S(2)}, u32[]{:S(2)}) collective-permute-start(bf16[8,128,128]{2,1,0:T(8,128)(2,1)S(1)} %get-tuple-element.46), channel_id=1, source_target_pairs={{0,16},{8,24},{16,32},{24,40},{32,48},{40,56},{48,64},{56,72},{64,... | collective-permute-start | bytes 786440 | tf_op jit(solution)/shard_map/ppermute | solution.py:28
  57.9 10.8 %collective-permute-start.6 = (bf16[8,128,128]{2,1,0:T(8,128)(2,1)S(1)}, bf16[8,128,128]{2,1,0:T(8,128)(2,1)S(1)}, u32[]{:S(2)}, u32[]{:S(2)}) collective-permute-start(bf16[8,128,128]{2,1,0:T(8,128)(2,1)S(1)} %get-tuple-element.47), channel_id=1, source_target_pairs={{0,248},{8,16},{16,8},{24,32},{32,24},{40,48},{48,40},{56,64},{64,... | collective-permute-start | bytes 786440 | tf_op jit(solution)/shard_map/ppermute | solution.py:38
  59.0 9.7 %collective-permute-start.7 = (bf16[8,128,128]{2,1,0:T(8,128)(2,1)S(1)}, bf16[8,128,128]{2,1,0:T(8,128)(2,1)S(1)}, u32[]{:S(2)}, u32[]{:S(2)}) collective-permute-start(bf16[8,128,128]{2,1,0:T(8,128)(2,1)S(1)} %get-tuple-element.48), channel_id=1, source_target_pairs={{0,8},{8,0},{16,24},{24,16},{32,40},{40,32},{48,56},{56,48},{64,72... | collective-permute-start | bytes 786440 | tf_op jit(solution)/shard_map/ppermute | solution.py:33

commit v2 on v1

--- a/solution.py
+++ b/solution.py
@@ -46,53 +46,91 @@
     return pltpu.VMEM(shape, dtype)
 
 
+def in_hbm(value):
+    return pltpu.with_memory_space_constraint(value, pltpu.HBM)
+
+
 def near(value):
     return pltpu.with_memory_space_constraint(value, pltpu.VMEM)
 
 
 SMEM = pl.BlockSpec(memory_space=pltpu.SMEM)
 VMEM = pl.BlockSpec(memory_space=pltpu.VMEM)
-
-
-def pack_kernel(owners, q_ref, g_ref, o_ref, k_ref, v_ref, out_ref):
+HBM = pl.BlockSpec(memory_space=pltpu.HBM)
+
+
+def pack_kernel(parts, q_in, g_in, o_in, k_in, v_in, out, out_ref, q_ref, g_ref, o_ref, k_ref, v_ref, sems):
     rows = q_ref.shape[0]
+    owners = out_ref.shape[0]
     width = GROUP * HEAD
     base = 2 * GROUP * rows
+    span = owners * width // parts
+    wide = []
+    for n in range(parts):
+        for m, (a, b) in enumerate(((g_in, g_ref), (o_in, o_ref), (q_in, q_ref))):
+            cols = pl.ds(n * span, span)
+            wide.append(pltpu.make_async_copy(a.at[:, cols], b.at[:, cols], sems.at[3 * n + m]))
+    narrow = [
+        pltpu.make_async_copy(k_in, k_ref, sems.at[3 * parts]),
+        pltpu.make_async_copy(v_in, v_ref, sems.at[3 * parts + 1]),
+    ]
+    for copy in wide[:3] + narrow + wide[3:]:
+        copy.start()
+    stores = []
     for n in range(owners):
-        deltas = []
+        if n % (owners // parts) == 0:
+            first = 3 * (n // (owners // parts))
+            for copy in wide[first : first + 3]:
+                copy.wait()
+        products = []
         for h in range(GROUP):
             cols = slice(n * width + h * HEAD, n * width + (h + 1) * HEAD)
             grad = g_ref[:, cols]
             out_ref[n, h * rows : (h + 1) * rows, :] = q_ref[:, cols]
             out_ref[n, (GROUP + h) * rows : (GROUP + h + 1) * rows, :] = grad
-            deltas.append(grad.astype(jnp.float32) * o_ref[:, cols].astype(jnp.float32))
-        lines = []
-        for h in range(0, GROUP, 2):
-            both = jnp.concatenate(deltas[h : h + 2], axis=0)
-            lines.append(jnp.sum(both.T, axis=0, keepdims=True))
-        delta = jnp.concatenate(lines, axis=0)
+            products.append(grad.astype(jnp.float32) * o_ref[:, cols].astype(jnp.float32))
+        products = jnp.concatenate(products, axis=0)
+        lead = products.astype(jnp.bfloat16)
+        rest = (products - lead.astype(jnp.float32)).astype(jnp.bfloat16)
+        ones = jnp.ones((8, HEAD), jnp.bfloat16)
+        across = (((1,), (1,)), ((), ()))
+        sums = lax.dot_general(ones, lead, across, preferred_element_type=jnp.float32)
+        sums += lax.dot_general(ones, rest, across, preferred_element_type=jnp.float32)
+        delta = jnp.concatenate([sums[0:1, :HEAD], sums[0:1, HEAD:]], axis=0)
         high = delta.astype(jnp.bfloat16).astype(jnp.float32)
         spare = jnp.zeros((DELTA_ROWS - GROUP, HEAD), jnp.float32)
         tile = jnp.concatenate([high, delta - high, spare], axis=0)
         out_ref[n, base : base + DELTA_ROWS, :] = tile.astype(jnp.bfloat16)
-        out_ref[n, base + DELTA_ROWS : base + DELTA_ROWS + rows, :] = k_ref[:, n * HEAD : (n + 1) * HEAD]
-        out_ref[n, base + DELTA_ROWS + rows :, :] = v_ref[:, n * HEAD : (n + 1) * HEAD]
+        if n == 0:
+            for copy in narrow:
+                copy.wait()
+        at = base + DELTA_ROWS
+        out_ref[n, at : at + rows, :] = k_ref[:, n * HEAD : (n + 1) * HEAD]
+        out_ref[n, at + rows :, :] = v_ref[:, n * HEAD : (n + 1) * HEAD]
+        if (n + 1) % (owners // parts) == 0:
+            here = pl.ds(n + 1 - owners // parts, owners // parts)
+            stores.append(pltpu.make_async_copy(out_ref.at[here], out.at[here], sems.at[3 * parts + 2 + len(stores)]))
+            stores[-1].start()
+    for copy in stores:
+        copy.wait()
 
 
 def pack(queries, keys, values, grads, outputs, heads):
     rows = queries.shape[0]
-    owners = 2
-    wide = pl.BlockSpec((rows, owners * GROUP * HEAD), lambda n: (0, n))
-    narrow = pl.BlockSpec((rows, owners * HEAD), lambda n: (0, n))
-    out_rows = (2 * GROUP + 2) * rows + DELTA_ROWS
+    parts = 2
+    args = (queries, grads, outputs, keys, values)
+    packed = (heads, (2 * GROUP + 2) * rows + DELTA_ROWS, HEAD)
     return pl.pallas_call(
-        functools.partial(pack_kernel, owners),
-        grid=(heads // owners,),
-        in_specs=[wide, wide, wide, narrow, narrow],
-        out_specs=pl.BlockSpec((owners, out_rows, HEAD), lambda n: (n, 0, 0)),
-        out_shape=jax.ShapeDtypeStruct((heads, out_rows, HEAD), jnp.bfloat16),
+        functools.partial(pack_kernel, parts),
+        in_specs=[HBM] * 5,
+        out_specs=HBM,
+        out_shape=jax.ShapeDtypeStruct(packed, jnp.bfloat16),
+        scratch_shapes=[pltpu.VMEM(packed, jnp.bfloat16)]
+        + [pltpu.VMEM(x.shape, x.dtype) for x in args]
+        + [pltpu.SemaphoreType.DMA((4 * parts + 2,))],
+        compiler_params=pltpu.CompilerParams(vmem_limit_bytes=24 * MIB),
         name="pack",
-    )(queries, grads, outputs, keys, values)
+    )(*[in_hbm(x) for x in args])
 
 
 def plan_kernel(seq_size, mine_ref, order_ref, start_ref, keep_ref, docs_ref):
@@ -133,7 +171,9 @@
     return tiles.reshape(BLK, HEAD)
 
 
-def near_kernel(rows, keep_ref, got_ref, pair_ref, e_ref, d_ref, qt_ref, gt_ref, u_ref, stat_ref, kv, scores):
+def near_kernel(
+    rows, keep_ref, got_ref, pair_ref, e_own, d_own, e_pair, d_pair, qt_ref, gt_ref, u_ref, stat_ref, kv, scores
+):
     per_block = BLK // rows
     chunk = GROUP * rows
     sources = 2 * per_block
@@ -154,7 +194,7 @@
             top = jnp.max(s, axis=0, keepdims=True)
             stat_ref[i, 0:1, lanes] = top if diagonal else jnp.maximum(top, stat_ref[i, 0:1, lanes])
 
-    def weigh(i, j, first):
+    def weigh(i, j, first, own):
         keys_t = block_of(kv, j, 0, rows).T
         values = block_of(kv, j, rows, rows)
         parts = []
@@ -165,8 +205,9 @@
             stat_ref[i, 1:2, lanes] = total if first else stat_ref[i, 1:2, lanes] + total
             dprobs = jnp.dot(values, gt_ref[i, :, lanes], preferred_element_type=jnp.float32)
             d = (e * (dprobs - stat_ref[i, 2:3, lanes])).astype(jnp.bfloat16)
-            e_ref[i * NEAR + j, :, lanes] = e.astype(jnp.bfloat16)
-            d_ref[i * NEAR + j, :, lanes] = d
+            e_ref, d_ref, at = (e_own, d_own, 2 * i + j) if own else (e_pair, d_pair, 2 * i + j - 2)
+            e_ref[at, :, lanes] = e.astype(jnp.bfloat16)
+            d_ref[at, :, lanes] = d
             parts.append(d)
         u = jnp.dot(keys_t, jnp.concatenate(parts, axis=1), preferred_element_type=jnp.float32)
         u_ref[i] = u if first else u_ref[i] + u
@@ -191,16 +232,20 @@
             return 0
 
         lax.fori_loop(0, NEAR, visit_scores, 0)
-        weigh(i, i, True)
+        weigh(i, i, True, True)
+
+        @pl.when(keep_ref[i * BLOCKS + 1 - i] == 1)
+        def _():
+            weigh(i, 1 - i, False, True)
 
         def visit_weights(j, _):
-            @pl.when((keep_ref[i * BLOCKS + j] == 1) & (j != i))
+            @pl.when(keep_ref[i * BLOCKS + j] == 1)
             def _():
-                weigh(i, j, False)
+                weigh(i, j, False, False)
 
             return 0
 
-        lax.fori_loop(0, NEAR, visit_weights, 0)
+        lax.fori_loop(2, NEAR, visit_weights, 0)
 
 
 def near_part(keep, got, pair, rows):
@@ -208,10 +253,9 @@
     return pl.pallas_call(
         functools.partial(near_kernel, rows),
         in_specs=[SMEM, VMEM, VMEM],
-        out_specs=[VMEM] * 6,
+        out_specs=[VMEM] * 8,
         out_shape=[
-            near_array((2 * NEAR, BLK, lanes), jnp.bfloat16),
-            near_array((2 * NEAR, BLK, lanes), jnp.bfloat16),
+            *[near_array((NEAR, BLK, lanes), jnp.bfloat16)] * 4,
             near_array((2, HEAD, lanes), jnp.bfloat16),
             near_array((2, HEAD, lanes), jnp.bfloat16),
             near_array((2, HEAD, lanes), jnp.float32),
@@ -229,7 +273,7 @@
 
 def far_kernel(
     rows, keep_ref, got_ref, before_ref, after_ref, cross_ref, e_ref, d_ref, qt_ref, gt_ref, u_ref,
-    stat_ref, to_before, to_after, to_cross, to_pair, out_ref, own_ref, kv, scores, acc, stats, dqt_ref, alpha_ref,
+    stat_ref, to_before, to_after, to_cross, to_pair, out_ref, alpha_ref, kv, scores, acc, stats, dqt_ref,
 ):
     per_block = BLK // rows
     chunk = GROUP * rows
@@ -271,7 +315,7 @@
             lanes = slice(c * chunk, (c + 1) * chunk)
             probs = jnp.exp2(scores[j, :, lanes] * SCALE2 - stats[2:3, lanes])
             dprobs = jnp.dot(values, gt_ref[i, :, lanes], preferred_element_type=jnp.float32)
-            all_d.append(((SCALE * probs) * (dprobs - stat_ref[i, 2:3, lanes])).astype(jnp.bfloat16))
+            all_d.append((probs * (dprobs - stat_ref[i, 2:3, lanes])).astype(jnp.bfloat16))
             all_p.append(probs.astype(jnp.bfloat16))
         probs = jnp.concatenate(all_p, axis=1)
         dscores = jnp.concatenate(all_d, axis=1)
@@ -281,8 +325,8 @@
         add(j, k, v)
 
     def pair_gradients(i, j):
-        p = (e_ref[i * NEAR + j].astype(jnp.float32) * alpha_ref[i, 0:1, :]).astype(jnp.bfloat16)
-        d = (d_ref[i * NEAR + j].astype(jnp.float32) * alpha_ref[i, 1:2, :]).astype(jnp.bfloat16)
+        p = (e_ref[2 * i + j].astype(jnp.float32) * alpha_ref[i, 0:1, :]).astype(jnp.bfloat16)
+        d = (d_ref[2 * i + j].astype(jnp.float32) * alpha_ref[i, 0:1, :]).astype(jnp.bfloat16)
         v = jnp.dot(p, queries_of(i, chunk), preferred_element_type=jnp.float32)
         k = jnp.dot(d, queries_of(i, 0), preferred_element_type=jnp.float32)
         add(far_blocks + j, k, v)
@@ -302,8 +346,7 @@
         stats[2:3, :] = lse
         alpha = jnp.exp2(stat_ref[i, 0:1, :] * SCALE2 - lse)
         alpha_ref[i, 0:1, :] = alpha
-        alpha_ref[i, 1:2, :] = alpha * SCALE
-        dqt_ref[i] = u_ref[i] * (alpha * SCALE)
+        dqt_ref[i] = u_ref[i] * alpha
 
         def visit_gradients(j, _):
             @pl.when(keep_ref[i * BLOCKS + NEAR + j] == 1)
@@ -315,21 +358,21 @@
         lax.fori_loop(0, far_blocks, visit_gradients, 0)
 
         def visit_pair(j, _):
-            @pl.when(keep_ref[i * BLOCKS + j] == 1)
+            @pl.when(keep_ref[i * BLOCKS + 2 + j] == 1)
             def _():
                 pair_gradients(i, j)
 
             return 0
 
-        lax.fori_loop(0, NEAR, visit_pair, 0)
+        lax.fori_loop(0, 2, visit_pair, 0)
         for c in range(per_block):
-            dq = dqt_ref[i, :, c * chunk : (c + 1) * chunk].T
+            dq = (dqt_ref[i, :, c * chunk : (c + 1) * chunk] * SCALE).T
             out_ref[i * per_block + c, :chunk, :] = dq.astype(jnp.bfloat16)
 
-    own_ref[...] = acc[3 * sources : 4 * sources]
-    for n, ref in enumerate((to_before, to_after, to_cross)):
-        ref[...] = acc[n * sources : (n + 1) * sources].astype(jnp.bfloat16)
-    to_pair[...] = acc[4 * sources :].astype(jnp.bfloat16)
+    for n, ref in enumerate((to_before, to_after, to_cross, to_pair)):
+        here = slice(n * sources, (n + 1) * sources)
+        ref[:, :rows, :] = (acc[here, :rows, :] * SCALE).astype(jnp.bfloat16)
+        ref[:, rows:, :] = acc[here, rows:, :].astype(jnp.bfloat16)
 
 
 def far_part(keep, got, before, after, cross, state, rows):
@@ -344,15 +387,14 @@
         out_shape=[
             *[jax.ShapeDtypeStruct((sources, tall, HEAD), jnp.bfloat16)] * 4,
             jax.ShapeDtypeStruct((sources, chunk + tall, HEAD), jnp.bfloat16),
-            jax.ShapeDtypeStruct((sources, tall, HEAD), jnp.float32),
+            jax.ShapeDtypeStruct((2, 8, lanes), jnp.float32),
         ],
         scratch_shapes=[
             pltpu.VMEM((3 * sources, tall, HEAD), jnp.bfloat16),
             pltpu.VMEM((BLOCKS - NEAR, BLK, lanes), jnp.float32),
-            pltpu.VMEM((5 * sources, tall, HEAD), jnp.float32),
+            pltpu.VMEM((4 * sources, tall, HEAD), jnp.float32),
             pltpu.VMEM((8, lanes), jnp.float32),
             pltpu.VMEM((2, HEAD, lanes), jnp.float32),
-            pltpu.VMEM((2, 8, lanes), jnp.float32),
         ],
         compiler_params=pltpu.CompilerParams(vmem_limit_bytes=24 * MIB),
         cost_estimate=pl.CostEstimate(flops=3_000_000_000, bytes_accessed=4_000_000, transcendentals=8_000_000),
@@ -360,34 +402,99 @@
     )(keep, got, before, after, cross, e, d, qt, gt, u, stat)
 
 
-def unpack_kernel(rows, got_ref, q_ref, k_ref, v_ref):
+def own_kernel(rows, keep_ref, got_ref, e_in, d_in, alpha_ref, own_ref, e_ref, d_ref, sems):
+    per_block = BLK // rows
+    chunk = GROUP * rows
+
+    def copies(n):
+        return (
+            pltpu.make_async_copy(e_in.at[n], e_ref.at[n], sems.at[n]),
+            pltpu.make_async_copy(d_in.at[n], d_ref.at[n], sems.at[NEAR + n]),
+        )
+
+    def when_kept(visit):
+        for i in range(2):
+            for j in range(2):
+                if i == j:
+                    visit(i, j)
+                else:
+                    pl.when(keep_ref[i * BLOCKS + j] == 1)(functools.partial(visit, i, j))
+
+    def load(i, j):
+        for copy in copies(2 * i + j):
+            copy.start()
+
+    def add(i, j):
+        for copy in copies(2 * i + j):
+            copy.wait()
+        p = (e_ref[2 * i + j].astype(jnp.float32) * alpha_ref[i, 0:1, :]).astype(jnp.bfloat16)
+        d = (d_ref[2 * i + j].astype(jnp.float32) * alpha_ref[i, 0:1, :]).astype(jnp.bfloat16)
+        tiles = got_ref[i * per_block : (i + 1) * per_block, : 2 * chunk, :]
+        q = tiles[:, :chunk, :].reshape(per_block * chunk, HEAD)
+        g = tiles[:, chunk:, :].reshape(per_block * chunk, HEAD)
+        v = jnp.dot(p, g, preferred_element_type=jnp.float32)
+        k = jnp.dot(d, q, preferred_element_type=jnp.float32) * SCALE
+        here = slice(j * per_block, (j + 1) * per_block)
+        own_ref[here, :rows, :] += k.reshape(per_block, rows, HEAD)
+        own_ref[here, rows:, :] += v.reshape(per_block, rows, HEAD)
+
+    when_kept(load)
+    own_ref[...] = jnp.zeros_like(own_ref)
+    when_kept(add)
+
+
+def own_part(keep, got, e, d, alpha, rows):
+    return pl.pallas_call(
+        functools.partial(own_kernel, rows),
+        in_specs=[SMEM, VMEM, HBM, HBM, VMEM],
+        out_specs=VMEM,
+        out_shape=jax.ShapeDtypeStruct((got.shape[0], 2 * rows, HEAD), jnp.float32),
+        scratch_shapes=[
+            pltpu.VMEM(e.shape, e.dtype),
+            pltpu.VMEM(d.shape, d.dtype),
+            pltpu.SemaphoreType.DMA((2 * NEAR,)),
+        ],
+        compiler_params=pltpu.CompilerParams(vmem_limit_bytes=16 * MIB),
+        cost_estimate=pl.CostEstimate(flops=1_000_000_000, bytes_accessed=4_000_000, transcendentals=0),
+        name="own_part",
+    )(keep, got, in_hbm(e), in_hbm(d), alpha)
+
+
+def unpack_kernel(rows, parts, got_ref, q_out, k_out, v_out, q_ref, k_ref, v_ref, sems):
+    owners = got_ref.shape[0]
     width = GROUP * HEAD
-    for n in range(got_ref.shape[0]):
+    copies = []
+    for n in range(owners):
         for h in range(GROUP):
             q_ref[:, n * width + h * HEAD : n * width + (h + 1) * HEAD] = got_ref[n, h * rows : (h + 1) * rows, :]
         k_ref[:, n * HEAD : (n + 1) * HEAD] = got_ref[n, GROUP * rows : (GROUP + 1) * rows, :]
         v_ref[:, n * HEAD : (n + 1) * HEAD] = got_ref[n, (GROUP + 1) * rows :, :]
+        if (n + 1) % (owners // parts) == 0:
+            span = owners * width // parts
+            cols = pl.ds((n + 1) * width - span, span)
+            copies.append(pltpu.make_async_copy(q_ref.at[:, cols], q_out.at[:, cols], sems.at[len(copies)]))
+            copies[-1].start()
+    copies.append(pltpu.make_async_copy(k_ref, k_out, sems.at[parts]))
+    copies.append(pltpu.make_async_copy(v_ref, v_out, sems.at[parts + 1]))
+    copies[-2].start()
+    copies[-1].start()
+    for copy in copies:
+        copy.wait()
 
 
 def unpack(got, rows):
     heads = got.shape[0]
-    owners = 4
+    parts = 4
+    shapes = [(rows, heads * GROUP * HEAD), (rows, heads * HEAD), (rows, heads * HEAD)]
     return pl.pallas_call(
-        functools.partial(unpack_kernel, rows),
-        grid=(heads // owners,),
-        in_specs=[pl.BlockSpec((owners,) + got.shape[1:], lambda n: (n, 0, 0))],
-        out_specs=[
-            pl.BlockSpec((rows, owners * GROUP * HEAD), lambda n: (0, n)),
-            pl.BlockSpec((rows, owners * HEAD), lambda n: (0, n)),
-            pl.BlockSpec((rows, owners * HEAD), lambda n: (0, n)),
-        ],
-        out_shape=[
-            jax.ShapeDtypeStruct((rows, heads * GROUP * HEAD), jnp.bfloat16),
-            jax.ShapeDtypeStruct((rows, heads * HEAD), jnp.bfloat16),
-            jax.ShapeDtypeStruct((rows, heads * HEAD), jnp.bfloat16),
-        ],
+        functools.partial(unpack_kernel, rows, parts),
+        in_specs=[VMEM],
+        out_specs=[HBM] * 3,
+        out_shape=[jax.ShapeDtypeStruct(x, jnp.bfloat16) for x in shapes],
+        scratch_shapes=[pltpu.VMEM(x, jnp.bfloat16) for x in shapes] + [pltpu.SemaphoreType.DMA((parts + 2,))],
+        compiler_params=pltpu.CompilerParams(vmem_limit_bytes=16 * MIB),
         name="unpack",
-    )(got)
+    )(near(got))
 
 
 def local(queries, keys, values, output_gradient, outputs, block_order, doc_start):
@@ -399,16 +506,17 @@
     got = swap_heads(pack(queries, keys, values, output_gradient, outputs, heads))
     kv = got[:, 2 * GROUP * rows + DELTA_ROWS :, :]
     kv, keep = lax.optimization_barrier((kv, keep))
+    cross, after, before = swap_cross(kv), send(kv, -REACH), send(kv, REACH)
     pair = swap_pair(kv)
-    before, after, cross = send(kv, REACH), send(kv, -REACH), swap_cross(kv)
     state = near_part(keep, near(got), near(pair), rows)
-    before, after, cross, *state = lax.optimization_barrier((before, after, cross, *state))
-    *sums, out, own = far_part(
+    e_own, d_own, *state = state
+    cross, after, before, *state = lax.optimization_barrier((cross, after, before, *state))
+    *sums, out, alpha = far_part(
         keep, near(got), near(before), near(after), near(cross), [near(x) for x in state], rows
     )
     to_before, to_after, to_cross, to_pair = sums
     back = (send(to_before, -REACH), send(to_after, REACH), swap_cross(to_cross), swap_pair(to_pair))
-    total = own
+    total = own_part(keep, got, e_own, d_own, alpha, rows)
     for part in back:
         total = total + part.astype(jnp.float32)
     out = lax.dynamic_update_slice(out, total.astype(jnp.bfloat16), (0, GROUP * rows, 0))

time: 85.8 us -> 83.6 us (0.974)
  waiting for transfers between devices: 32.8 us -> 22.5 us
  starting transfers between devices: 20.4 us -> 26.4 us
  local copies, waits for them, and re-layouts: 0.67 us -> 3.33 us
    ppermute x4, waiting for transfers between devices: 14 us -> 0.01 us  [send(): lax.ppermute(value, 'seq', [(i, (i + steps) % count) for i in range(count)])]
    ppermute x2, waiting for transfers between devices: 0.1 us -> 3.74 us  [swap_cross(): lax.ppermute(value, 'seq', [(i, (i + (1 if i % 2 else count - 1)) % count...]
    ppermute x4, starting transfers between devices: 6.35 us -> 9.94 us  [send(): lax.ppermute(value, 'seq', [(i, (i + steps) % count) for i in range(count)])]
    pallas_call x1, Pallas kernels: 5.16 us -> 2.4 us  [far_part(): pl.pallas_call(functools.partial(far_kernel, rows), in_specs=[SMEM] + [VM...]
    unnamed x2 -> x6, local copies, waits for them, and re-layouts: 0.66 us -> 3.31 us
    ppermute x2, starting transfers between devices: 7.95 us -> 10.3 us  [swap_cross(): lax.ppermute(value, 'seq', [(i, (i + (1 if i % 2 else count - 1)) % count...]
    pallas_call x1, Pallas kernels: 3.37 us -> 4.98 us  [near_part(): pl.pallas_call(functools.partial(near_kernel, rows), in_specs=[SMEM, VMEM...]
    pallas_call x2 -> x3, Pallas kernels: 5.86 us -> 6.87 us  [the longest x1 3.09 us: own_part(): pl.pallas_call(functools.partial(own_kernel, rows), in_specs=[SMEM, VMEM,...]
  transfers between devices with their start and end apart: 9 -> 9, of which waited for: 6 -> 2; matrix products, arithmetic and copies ran while one was open for 0% -> 0% of each run, Pallas kernels for 6% -> 12%
where the time goes in v2:
time: 83.6 us; the launch traced here: 83.4 us
  starting transfers between devices  26.4 us (32%)
  waiting for transfers between devices  22.5 us (27%)
  Pallas kernels  15.9 us (19%)
  blocking collectives  14.3 us (17%)
  local copies, waits for them, and re-layouts  3.33 us (4%)
  between operations  0.88 us (1%)
    all_to_all x1, waiting for transfers between devices, swap_heads(): lax.all_to_all(value, 'head', split_axis=0, concat_axis=0, tiled=True)  18.8 us
    all_to_all x1, blocking collectives, swap_heads(): lax.all_to_all(value, 'head', split_axis=0, concat_axis=0, tiled=True)  14.3 us
    ppermute x2, starting transfers between devices, swap_cross(): lax.ppermute(value, 'seq', [(i, (i + (1 if i % 2 else count - 1)) % count...  10.3 us
    ppermute x4, starting transfers between devices, send(): lax.ppermute(value, 'seq', [(i, (i + steps) % count) for i in range(count)])  9.94 us
    all_to_all x1, starting transfers between devices, swap_heads(): lax.all_to_all(value, 'head', split_axis=0, concat_axis=0, tiled=True)  6.04 us
    pallas_call x1, Pallas kernels, near_part(): pl.pallas_call(functools.partial(near_kernel, rows), in_specs=[SMEM, VMEM...  4.98 us
    ppermute x2, waiting for transfers between devices, swap_cross(): lax.ppermute(value, 'seq', [(i, (i + (1 if i % 2 else count - 1)) % count...  3.74 us
    unnamed x6, local copies, waits for them, and re-layouts  3.31 us
  transfers between devices with their start and end apart: 9, of which 2 were waited for; matrix products, arithmetic and copies ran while one was open for 0% of the time, Pallas kernels for 12%

profile of v2, /device:TPU:2, one launch (start us, length us, event | category | flops | bytes accessed | tf_op | source)
XLA Modules:
  0.0 83.4 jit_solution(12510391445043571467)
XLA Ops:
  0.6 2.8 %pack.1 = bf16[8,656,128]{2,1,0:T(8,128)(2,1)} custom-call(bf16[64,4096]{1,0:T(8,128)(2,1)} %q_in.1, bf16[64,4096]{1,0:T(8,128)(2,1)} %g_in.1, bf16[64,4096]{1,0:T(8,128)(2,1)} %o_in.1, bf16[64,1024]{1,0:T(8,128)(2,1)} %k_in.1, bf16[64,1024]{1,0:T(8,128)(2,1)} %v_in.1), custom_call_target="tpu_custom_call" | custom-call | tf_op jit(solution)/shard_map/pack/pallas_call | solution.py:123
  3.5 6.0 %all-to-all-start = ((bf16[8,656,128]{2,1,0:T(8,128)(2,1)}), bf16[8,656,128]{2,1,0:T(8,128)(2,1)S(1)}, u32[]{:S(2)}, u32[]{:S(2)}) async-start(bf16[8,656,128]{2,1,0:T(8,128)(2,1)} %pack.1), calls=%async_computation | async-start | bytes 2686976 | tf_op jit(solution)/shard_map/all_to_all | solution.py:42
  9.5 1.6 %plan.1.keep_ref = s32[20]{0:T(128)} custom-call(s32[1]{0:T(128)} %bitcast.mine_ref, s32[64]{0:T(128)} %order_ref.1, s32[64]{0:T(128)} %start_ref.1), custom_call_target="tpu_custom_call" | custom-call | tf_op jit(solution)/shard_map/plan/pallas_call | solution.py:158
  11.2 18.8 %all-to-all-done.got_ref = bf16[8,656,128]{2,1,0:T(8,128)(2,1)S(1)} async-done(((bf16[8,656,128]{2,1,0:T(8,128)(2,1)}), bf16[8,656,128]{2,1,0:T(8,128)(2,1)S(1)}, u32[]{:S(2)}, u32[]{:S(2)}) %all-to-all-start) | async-done | bytes 1343520 | tf_op jit(solution)/shard_map/all_to_all | solution.py:42
  29.9 0.1 collective-permute-start.3
  30.0 2.0 %collective-permute-start.2 = (bf16[8,128,128]{2,1,0:T(8,128)(2,1)S(1)}, bf16[8,128,128]{2,1,0:T(8,128)(2,1)S(1)}, u32[]{:S(2)}, u32[]{:S(2)}) collective-permute-start(bf16[8,128,128]{2,1,0:T(8,128)(2,1)S(1)} %slice.4), channel_id=1, source_target_pairs={{0,16},{8,24},{16,32},{24,40},{32,48},{40,56},{48,64},{56,72},{64,... | collective-permute-start | bytes 786440 | tf_op jit(solution)/shard_map/ppermute | solution.py:28
  32.0 4.9 %collective-permute-start.1 = (bf16[8,128,128]{2,1,0:T(8,128)(2,1)S(1)}, bf16[8,128,128]{2,1,0:T(8,128)(2,1)S(1)}, u32[]{:S(2)}, u32[]{:S(2)}) collective-permute-start(bf16[8,128,128]{2,1,0:T(8,128)(2,1)S(1)} %slice.4), channel_id=1, source_target_pairs={{0,240},{8,248},{16,0},{24,8},{32,16},{40,24},{48,32},{56,40},{64,... | collective-permute-start | bytes 786440 | tf_op jit(solution)/shard_map/ppermute | solution.py:28
  36.9 1.4 %collective-permute-start = (bf16[8,128,128]{2,1,0:T(8,128)(2,1)S(1)}, bf16[8,128,128]{2,1,0:T(8,128)(2,1)S(1)}, u32[]{:S(2)}, u32[]{:S(2)}) collective-permute-start(bf16[8,128,128]{2,1,0:T(8,128)(2,1)S(1)} %slice.4), channel_id=1, source_target_pairs={{0,248},{8,16},{16,8},{24,32},{32,24},{40,48},{48,40},{56,64},{64,... | collective-permute-start | bytes 786440 | tf_op jit(solution)/shard_map/ppermute | solution.py:38
  38.4 0.0 collective-permute-done.3.pair_ref
  38.4 0.7 copy-done.2
  39.0 5.0 %near_part.1 = (bf16[4,256,1024]{2,1,0:T(8,128)(2,1)S(1)}, bf16[4,256,1024]{2,1,0:T(8,128)(2,1)S(1)}, bf16[4,256,1024]{2,1,0:T(8,128)(2,1)S(1)}, bf16[4,256,1024...) custom-call(s32[20]{0:T(128)S(1)} %copy-done.2, ...), custom_call_target="tpu_custom_call" | custom-call | flops 3000000000 | bytes 4000000 | tf_op jit(solution)/shard_map/near_part/pallas_call | solution.py:253
  44.0 1.3 %copy-done = bf16[4,256,1024]{2,1,0:T(8,128)(2,1)} copy-done((bf16[4,256,1024]{2,1,0:T(8,128)(2,1)}, bf16[4,256,1024]{2,1,0:T(8,128)(2,1)S(1)}, u32[]{:S(2)}) %copy-start) | copy-done | bytes 2097176
  45.3 1.3 %copy-done.1 = bf16[4,256,1024]{2,1,0:T(8,128)(2,1)} copy-done((bf16[4,256,1024]{2,1,0:T(8,128)(2,1)}, bf16[4,256,1024]{2,1,0:T(8,128)(2,1)S(1)}, u32[]{:S(2)}) %copy-start.1) | copy-done | bytes 2097176
  46.7 0.0 collective-permute-done.2.before_ref
  46.7 0.0 collective-permute-done.1.after_ref
  46.7 0.0 collective-permute-done.cross_ref
  46.7 2.4 %far_part.1 = (bf16[8,128,128]{2,1,0:T(8,128)(2,1)S(1)}, bf16[8,128,128]{2,1,0:T(8,128)(2,1)S(1)}, bf16[8,128,128]{2,1,0:T(8,128)(2,1)S(1)}, bf16[8,128,128]{2,1...) custom-call(s32[20]{0:T(128)S(1)} %copy-done.2, ...), custom_call_target="tpu_custom_call" | custom-call | flops 3000000000 | bytes 4000000 | tf_op jit(solution)/shard_map/far_part/pallas_call | solution.py:383
  49.1 3.1 %collective-permute-start.4 = (bf16[8,128,128]{2,1,0:T(8,128)(2,1)S(1)}, bf16[8,128,128]{2,1,0:T(8,128)(2,1)S(1)}, u32[]{:S(2)}, u32[]{:S(2)}) collective-permute-start(bf16[8,128,128]{2,1,0:T(8,128)(2,1)S(1)} %get-tuple-element.49), channel_id=1, source_target_pairs={{0,240},{8,248},{16,0},{24,8},{32,16},{40,24},{48,32},{56,40},{64,... | collective-permute-start | bytes 786440 | tf_op jit(solution)/shard_map/ppermute | solution.py:28
  52.1 8.9 %collective-permute-start.6 = (bf16[8,128,128]{2,1,0:T(8,128)(2,1)S(1)}, bf16[8,128,128]{2,1,0:T(8,128)(2,1)S(1)}, u32[]{:S(2)}, u32[]{:S(2)}) collective-permute-start(bf16[8,128,128]{2,1,0:T(8,128)(2,1)S(1)} %get-tuple-element.51), channel_id=1, source_target_pairs={{0,248},{8,16},{16,8},{24,32},{32,24},{40,48},{48,40},{56,64},{64,... | collective-permute-start | bytes 786440 | tf_op jit(solution)/shard_map/ppermute | solution.py:38
  61.0 3.1 %own_part.1 = f32[8,128,128]{2,1,0:T(8,128)S(1)} custom-call(s32[20]{0:T(128)S(1)} %copy-done.2, bf16[8,656,128]{2,1,0:T(8,128)(2,1)S(1)} %all-to-all-done.got_ref, bf16[4,256,1024]{2,1,0:T(8,128)(2,1)} %copy-done, bf16[4,256,1024]{2,1,0:T(8,128)(2,1)} %copy-done.1, f32[2,8,1024]{2,1,0:T(8,128)S(1)} %get-tuple-element.48.alpha_ref), custom_call_target="tpu_custom_call" | custom-call | flops 1000000000 | bytes 4000000 | tf_op jit(solution)/shard_map/own_part/pallas_call | solution.py:447
  64.1 3.7 %collective-permute-done.6 = bf16[8,128,128]{2,1,0:T(8,128)(2,1)S(1)} collective-permute-done((bf16[8,128,128]{2,1,0:T(8,128)(2,1)S(1)}, bf16[8,128,128]{2,1,0:T(8,128)(2,1)S(1)}, u32[]{:S(2)}, u32[]{:S(2)}) %collective-permute-start.6) | collective-permute-done | bytes 262176 | tf_op jit(solution)/shard_map/ppermute | solution.py:38
  67.9 0.2 fusion
  68.1 14.3 %all_to_all.10.got_ref = bf16[8,384,128]{2,1,0:T(8,128)(2,1)S(1)} all-to-all(bf16[8,384,128]{2,1,0:T(8,128)(2,1)S(1)} %fusion), channel_id=1, replica_groups=mesh['seq'=32,'head'=8] {'head'}, dimensions={0} | all-to-all | bytes 1572864 | tf_op jit(solution)/shard_map/all_to_all | solution.py:42
  82.3 0.9 %unpack.1 = (bf16[64,4096]{1,0:T(8,128)(2,1)}, bf16[64,1024]{1,0:T(8,128)(2,1)}, bf16[64,1024]{1,0:T(8,128)(2,1)}) custom-call(bf16[8,384,128]{2,1,0:T(8,128)(2,1)S(1)} %all_to_all.10.got_ref), custom_call_target="tpu_custom_call" | custom-call | tf_op jit(solution)/shard_map/unpack/pallas_call | solution.py:489
  (9 shorter events, 0.0 us)
Async XLA Ops:
  3.5 26.4 %all-to-all-start = ((bf16[8,656,128]{2,1,0:T(8,128)(2,1)}), bf16[8,656,128]{2,1,0:T(8,128)(2,1)S(1)}, u32[]{:S(2)}, u32[]{:S(2)}) async-start(bf16[8,656,128]{2,1,0:T(8,128)(2,1)} %pack.1), calls=%async_computation | async-start | bytes 2686976 | tf_op jit(solution)/shard_map/all_to_all | solution.py:42
  29.9 8.4 %collective-permute-start.3 = (bf16[8,128,128]{2,1,0:T(8,128)(2,1)S(1)}, bf16[8,128,128]{2,1,0:T(8,128)(2,1)S(1)}, u32[]{:S(2)}, u32[]{:S(2)}) collective-permute-start(bf16[8,128,128]{2,1,0:T(8,128)(2,1)S(1)} %slice.4), channel_id=1, source_target_pairs={{0,8},{8,0},{16,24},{24,16},{32,40},{40,32},{48,56},{56,48},{64,72... | collective-permute-start | bytes 786440 | tf_op jit(solution)/shard_map/ppermute | solution.py:33
  30.0 16.6 %collective-permute-start.2 = (bf16[8,128,128]{2,1,0:T(8,128)(2,1)S(1)}, bf16[8,128,128]{2,1,0:T(8,128)(2,1)S(1)}, u32[]{:S(2)}, u32[]{:S(2)}) collective-permute-start(bf16[8,128,128]{2,1,0:T(8,128)(2,1)S(1)} %slice.4), channel_id=1, source_target_pairs={{0,16},{8,24},{16,32},{24,40},{32,48},{40,56},{48,64},{56,72},{64,... | collective-permute-start | bytes 786440 | tf_op jit(solution)/shard_map/ppermute | solution.py:28
  32.0 14.6 %collective-permute-start.1 = (bf16[8,128,128]{2,1,0:T(8,128)(2,1)S(1)}, bf16[8,128,128]{2,1,0:T(8,128)(2,1)S(1)}, u32[]{:S(2)}, u32[]{:S(2)}) collective-permute-start(bf16[8,128,128]{2,1,0:T(8,128)(2,1)S(1)} %slice.4), channel_id=1, source_target_pairs={{0,240},{8,248},{16,0},{24,8},{32,16},{40,24},{48,32},{56,40},{64,... | collective-permute-start | bytes 786440 | tf_op jit(solution)/shard_map/ppermute | solution.py:28
  36.9 9.7 %collective-permute-start = (bf16[8,128,128]{2,1,0:T(8,128)(2,1)S(1)}, bf16[8,128,128]{2,1,0:T(8,128)(2,1)S(1)}, u32[]{:S(2)}, u32[]{:S(2)}) collective-permute-start(bf16[8,128,128]{2,1,0:T(8,128)(2,1)S(1)} %slice.4), channel_id=1, source_target_pairs={{0,248},{8,16},{16,8},{24,32},{32,24},{40,48},{48,40},{56,64},{64,... | collective-permute-start | bytes 786440 | tf_op jit(solution)/shard_map/ppermute | solution.py:38
  38.4 0.7 copy-start.2
  44.0 1.3 %copy-start = (bf16[4,256,1024]{2,1,0:T(8,128)(2,1)}, bf16[4,256,1024]{2,1,0:T(8,128)(2,1)S(1)}, u32[]{:S(2)}) copy-start(bf16[4,256,1024]{2,1,0:T(8,128)(2,1)S(1)} %get-tuple-element.46.e_in) | copy-start | bytes 6291460
  45.3 1.3 %copy-start.1 = (bf16[4,256,1024]{2,1,0:T(8,128)(2,1)}, bf16[4,256,1024]{2,1,0:T(8,128)(2,1)S(1)}, u32[]{:S(2)}) copy-start(bf16[4,256,1024]{2,1,0:T(8,128)(2,1)S(1)} %get-tuple-element.47.d_in) | copy-start | bytes 6291460
  49.1 15.0 %collective-permute-start.4 = (bf16[8,128,128]{2,1,0:T(8,128)(2,1)S(1)}, bf16[8,128,128]{2,1,0:T(8,128)(2,1)S(1)}, u32[]{:S(2)}, u32[]{:S(2)}) collective-permute-start(bf16[8,128,128]{2,1,0:T(8,128)(2,1)S(1)} %get-tuple-element.49), channel_id=1, source_target_pairs={{0,240},{8,248},{16,0},{24,8},{32,16},{40,24},{48,32},{56,40},{64,... | collective-permute-start | bytes 786440 | tf_op jit(solution)/shard_map/ppermute | solution.py:28
  52.1 12.0 %collective-permute-start.5 = (bf16[8,128,128]{2,1,0:T(8,128)(2,1)S(1)}, bf16[8,128,128]{2,1,0:T(8,128)(2,1)S(1)}, u32[]{:S(2)}, u32[]{:S(2)}) collective-permute-start(bf16[8,128,128]{2,1,0:T(8,128)(2,1)S(1)} %get-tuple-element.50), channel_id=1, source_target_pairs={{0,16},{8,24},{16,32},{24,40},{32,48},{40,56},{48,64},{56,72},{64,... | collective-permute-start | bytes 786440 | tf_op jit(solution)/shard_map/ppermute | solution.py:28
  52.1 15.7 %collective-permute-start.6 = (bf16[8,128,128]{2,1,0:T(8,128)(2,1)S(1)}, bf16[8,128,128]{2,1,0:T(8,128)(2,1)S(1)}, u32[]{:S(2)}, u32[]{:S(2)}) collective-permute-start(bf16[8,128,128]{2,1,0:T(8,128)(2,1)S(1)} %get-tuple-element.51), channel_id=1, source_target_pairs={{0,248},{8,16},{16,8},{24,32},{32,24},{40,48},{48,40},{56,64},{64,... | collective-permute-start | bytes 786440 | tf_op jit(solution)/shard_map/ppermute | solution.py:38
  61.0 6.9 %collective-permute-start.7 = (bf16[8,128,128]{2,1,0:T(8,128)(2,1)S(1)}, bf16[8,128,128]{2,1,0:T(8,128)(2,1)S(1)}, u32[]{:S(2)}, u32[]{:S(2)}) collective-permute-start(bf16[8,128,128]{2,1,0:T(8,128)(2,1)S(1)} %get-tuple-element.52), channel_id=1, source_target_pairs={{0,8},{8,0},{16,24},{24,16},{32,40},{40,32},{48,56},{56,48},{64,72... | collective-permute-start | bytes 786440 | tf_op jit(solution)/shard_map/ppermute | solution.py:33
